TPU v7x, 512 devices: a whole 4x8x8 slice. The times are simulated.
512 devices in a mesh: row: 16 (over z, core), col: 32 (over y, x).
Axes of the slice: x: 4, y: 8, z: 8, core: 2. Of those that a mesh axis runs over, the one named last changes fastest.
Arguments:
- velocity: bfloat16 [3, 4, 4224, 4096], P(None, None, 'row', 'col'), may hold values from -6 to 6
- rhs_prev: bfloat16 [3, 4, 4224, 4096], P(None, None, 'row', 'col'), may hold values from -12 to 12
- row_counts: int32 [16], replicated, may hold values from 248 to 264, as said below
- x_scale: float32 [4096], P('col'), may hold values from 0.5 to 2
- x_curv: float32 [4096], P('col'), may hold values from -3 to 3
- y_scale: float32 [4224], P('row'), may hold values from 0.5 to 12
- y_curv: float32 [4224], P('row'), may hold values from -3 to 3
- x_local: bfloat16 [132, 2, 128], replicated, may hold values from -0.5 to 0.5
- x_coupling: float32 [2, 64, 64], replicated, may hold values from -0.75 to 0.75
- x_basis: float32 [2, 2, 128], replicated, may hold values from -3 to 3
- y_local: bfloat16 [4288, 2, 264], P('row'), may hold values from -0.375 to 0.375
- y_coupling: float32 [2, 32, 32], replicated, may hold values from -1 to 1
- y_basis: float32 [16, 2, 2, 264], P('row'), may hold values from -3 to 3
Outputs:
- rhs: bfloat16 [3, 4, 4224, 4096], P(None, None, 'row', 'col')
- increment: bfloat16 [3, 4, 4224, 4096], P(None, None, 'row', 'col')
Inputs may be any that keep to these rules, and one draw needn't show every extreme that they name: `row_counts`: the counts sum to 4097; each is at least 2, and the largest is exactly 264.
All inputs are finite; a program needn't handle non-finite values.
Results may differ from a plain program's by a relative error of at most 0.0055.
Values may be sent and summed in bfloat16 or wider, within the bound.
No kernel may reach another device: no remote copies, remote signals or barrier semaphores. Data moves between devices by JAX's collectives and lax.ppermute only.
A program may use at most 64 MiB of HBM per device.

v0:
```python
import jax
import jax.numpy as jnp
from jax import lax
from jax.sharding import Mesh
from jax.sharding import PartitionSpec as P

COL = ("col_0", "col_1")
ROW = ("row_0", "row_1")
ROW_COL = ("row_0", "row_1", "col_0", "col_1")


viscosity = 0.1
cfl_target = 1.5
gamma_coef = 5.0 / 12.0
zeta_coef = -17.0 / 60.0


def by_axis(value, axes):
    for axis in axes:
        value = lax.pmax(value, axis)
    return value


def padded_2(block, sides, width, periodic):
    for axis, dim in sides:
        count = lax.axis_size(axis)
        forward = [(i, i + 1) for i in range(count - 1)]
        if periodic:
            forward.append((count - 1, 0))
        backward = [(target, source) for source, target in forward]
        low = lax.ppermute(
            lax.slice_in_dim(block, block.shape[dim] - width, None, axis=dim), axis, forward
        )
        high = lax.ppermute(lax.slice_in_dim(block, 0, width, axis=dim), axis, backward)
        block = jnp.concatenate([low, block, high], axis=dim)
    return block


def in_order(tiles, dim):
    dims = list(tiles.shape[1:])
    dims[dim] *= tiles.shape[0]
    return jnp.moveaxis(tiles, 0, dim).reshape(dims)


def copy_for_each(value, axis):
    length = lax.axis_size(axis)
    return lax.all_to_all(
        jnp.broadcast_to(value[None], (length, *value.shape)), axis, 0, 0, tiled=True
    )


def gather_directly(value, axis, dim):
    return in_order(copy_for_each(value, axis), dim)


def shards(
    velocity,
    rhs_prev,
    row_counts,
    x_scale,
    x_curv,
    y_scale,
    y_curv,
    x_local,
    x_coupling,
    x_basis,
    y_local,
    y_coupling,
    y_basis,
):
    n_comp, n_plane, y_rows, x_width = velocity.shape
    col_pos = lax.axis_index(COL)
    row_pos = lax.axis_index(ROW)
    own_count = row_counts[row_pos]
    slot_ids = jnp.arange(y_rows, dtype=jnp.int32)
    valid_rows = slot_ids < own_count
    speeds = (
        jnp.abs(velocity[0].astype(jnp.float32)) * x_scale
        + jnp.abs(velocity[1].astype(jnp.float32)) * y_scale[:, None]
    )
    local_top = jnp.max(jnp.where(valid_rows[:, None], speeds, jnp.float32(0.0)))
    speed_top = by_axis(local_top, ROW_COL)
    time_step = cfl_target / (speed_top + 1e-06)
    line_rows = velocity.reshape(n_comp * n_plane * y_rows, x_width)
    line_count = line_rows.shape[0]
    padded = padded_2(line_rows, ((COL, 1),), 2, True)
    local_x = jnp.dot(
        padded, x_local.reshape(x_width + 4, 2 * x_width), preferred_element_type=jnp.float32
    )
    ends_x = jnp.stack(
        [
            jnp.stack([local_x[:, 0], local_x[:, x_width]]),
            jnp.stack([local_x[:, x_width - 1], local_x[:, 2 * x_width - 1]]),
        ]
    )
    every_end = gather_directly(ends_x.astype(jnp.bfloat16), COL, 0).astype(ends_x.dtype)
    own_rows = lax.dynamic_slice_in_dim(x_coupling, 2 * col_pos, 2, 1)
    solved_x = jnp.einsum("kim,mkl->ikl", own_rows, every_end, precision=lax.Precision.HIGHEST)
    result_x = (
        local_x.reshape(line_count, 2, x_width)
        + jnp.transpose(solved_x[0])[:, :, None] * x_basis[:, 0, :]
        + jnp.transpose(solved_x[1])[:, :, None] * x_basis[:, 1, :]
    )
    first_x = result_x[:, 0].reshape(n_comp, n_plane, y_rows, x_width)
    second_x = result_x[:, 1].reshape(n_comp, n_plane, y_rows, x_width)
    columns = n_comp * n_plane * x_width
    stacked = jnp.transpose(velocity, (2, 0, 1, 3)).reshape(y_rows, columns)
    stacked = jnp.where(valid_rows[:, None], stacked, jnp.zeros((), jnp.bfloat16))
    edge_rows = jnp.concatenate(
        [stacked[0:2], lax.dynamic_slice_in_dim(stacked, own_count - 2, 2, 0)], axis=0
    )
    rimmed = padded_2(edge_rows, ((ROW, 0),), 2, False)
    extended = jnp.concatenate([rimmed[0:2], stacked, rimmed[6:8]], axis=0)
    local_y = lax.dot_general(
        y_local.reshape(y_rows + 4, 2 * y_rows),
        extended,
        (((0,), (0,)), ((), ())),
        preferred_element_type=jnp.float32,
    )
    local_y = local_y.reshape(2, y_rows, columns)
    first_rows = local_y[:, 0, :]
    last_rows = lax.dynamic_index_in_dim(local_y, own_count - 1, 1, keepdims=False)
    ends_y = jnp.stack([first_rows, last_rows])
    every_end = gather_directly(ends_y, ROW, 0)
    own_rows = lax.dynamic_slice_in_dim(y_coupling, 2 * row_pos, 2, 1)
    solved_y = jnp.einsum("kim,mkl->ikl", own_rows, every_end, precision=lax.Precision.HIGHEST)
    basis_y = y_basis[0]
    result_y = (
        local_y
        + solved_y[0][:, None, :] * basis_y[:, 0, :, None]
        + solved_y[1][:, None, :] * basis_y[:, 1, :, None]
    )
    first_y = jnp.transpose(result_y[0].reshape(y_rows, n_comp, n_plane, x_width), (1, 2, 0, 3))
    second_y = jnp.transpose(result_y[1].reshape(y_rows, n_comp, n_plane, x_width), (1, 2, 0, 3))
    scale_y = y_scale[:, None]
    curve_y = y_curv[:, None]
    velocity_f = velocity.astype(jnp.float32)
    grad_x = x_scale * first_x
    grad_y = scale_y * first_y
    laplacian = (
        x_scale * x_scale * second_x
        + x_curv * first_x
        + scale_y * scale_y * second_y
        + curve_y * first_y
    )
    rhs_full = -(velocity_f[0:1] * grad_x + velocity_f[1:2] * grad_y) + viscosity * laplacian
    live_mask = valid_rows[None, None, :, None]
    rhs_full = jnp.where(live_mask, rhs_full, jnp.float32(0.0))
    change = time_step * (gamma_coef * rhs_full + zeta_coef * rhs_prev.astype(jnp.float32))
    change = jnp.where(live_mask, change, jnp.float32(0.0))
    return (rhs_full.astype(jnp.bfloat16), change.astype(jnp.bfloat16))


def solution(mesh):
    torus = Mesh(mesh.devices.reshape(8, 2, 8, 4), ("row_0", "row_1", "col_0", "col_1"))
    placed = (
        P(None, None, ROW, COL),
        P(None, None, ROW, COL),
        P(),
        P(COL),
        P(COL),
        P(ROW),
        P(ROW),
        P(),
        P(),
        P(),
        P(ROW, None, None),
        P(),
        P(ROW, None, None, None),
    )
    return jax.shard_map(
        shards,
        mesh=torus,
        in_specs=placed,
        out_specs=(P(None, None, ROW, COL), P(None, None, ROW, COL)),
        check_vma=False,
    )
```

profile of v0, /device:TPU:1, one launch (start us, length us, event | category | flops | bytes accessed | tf_op | source)
XLA Modules:
  0.0 151.5 jit_solution(14803651987767590616)
XLA Ops:
  0.6 1.8 %fusion.30 = (bf16[3168,2]{1,0:T(8,128)(2,1)S(1)}, bf16[3168,2]{1,0:T(8,128)(2,1)S(1)}) fusion(bf16[3168,128]{1,0:T(8,128)(2,1)} %bitcast.102), kind=kLoop, calls=%fused_computation.61 | loop fusion | bytes 50688 | tf_op jit(solution)/shard_map/slice | solution.py:32
  2.4 0.3 copy.41
  2.8 4.0 %collective-permute-start = (bf16[3168,2]{0,1:T(2,128)(2,1)S(1)}, bf16[3168,2]{0,1:T(2,128)(2,1)S(1)}, u32[]{:S(2)}, u32[]{:S(2)}) collective-permute-start(bf16[3168,2]{0,1:T(2,128)(2,1)S(1)} %copy.41), channel_id=1, source_target_pairs={{0,1},{1,2},{2,3},{3,4},{4,5},{5,6},{6,7},{7,8},{8,9},{9,10},{10,1... | collective-permute-start | bytes 38024 | tf_op jit(solution)/shard_map/ppermute | solution.py:31
  6.7 0.3 copy.42
  7.1 6.1 %collective-permute-start.1 = (bf16[3168,2]{0,1:T(2,128)(2,1)S(1)}, bf16[3168,2]{0,1:T(2,128)(2,1)S(1)}, u32[]{:S(2)}, u32[]{:S(2)}) collective-permute-start(bf16[3168,2]{0,1:T(2,128)(2,1)S(1)} %copy.42), channel_id=1, source_target_pairs={{1,0},{2,1},{3,2},{4,3},{5,4},{6,5},{7,6},{8,7},{9,8},{10,9},{11,1... | collective-permute-start | bytes 38024 | tf_op jit(solution)/shard_map/ppermute | solution.py:34
  13.2 0.6 dynamic_slice.16
  13.8 0.6 iota_compare_fusion
  15.5 0.3 copy.48
  15.8 0.3 reshape.83
  16.3 0.9 copy-done.4
  17.2 0.6 constant_dynamic-slice_fusion
  17.8 4.8 %collective-permute-start.2 = (bf16[2,1536]{1,0:T(2,128)(2,1)}, bf16[2,1536]{1,0:T(2,128)(2,1)S(1)}, u32[]{:S(2)}, u32[]{:S(2)}) collective-permute-start(bf16[2,1536]{1,0:T(2,128)(2,1)} %get-tuple-element.20), channel_id=1, source_target_pairs={{0,32},{32,64},{64,96},{96,128},{128,160},{160,192},{192,224},{224... | collective-permute-start | bytes 18440 | tf_op jit(solution)/shard_map/ppermute | solution.py:31
  22.7 0.8 fusion.20
  23.5 4.3 %collective-permute-start.3 = (bf16[2,1536]{1,0:T(2,128)(2,1)}, bf16[2,1536]{1,0:T(2,128)(2,1)S(1)}, u32[]{:S(2)}, u32[]{:S(2)}) collective-permute-start(bf16[2,1536]{1,0:T(2,128)(2,1)} %get-tuple-element.21), channel_id=1, source_target_pairs={{32,0},{64,32},{96,64},{128,96},{160,128},{192,160},{224,192},{256... | collective-permute-start | bytes 18440 | tf_op jit(solution)/shard_map/ppermute | solution.py:34
  27.8 15.7 %pmax.28 = f32[]{:T(128)} all-reduce(f32[]{:T(128)} %fusion.20), channel_id=1, replica_groups=mesh['row_0'=8,'row_1'=2,'col_0'=8,'col_1'=4] {'row_0'}, use_global_device_ids=true, to_apply=%region_1.2 | all-reduce | flops 1 | bytes 8 | tf_op jit(solution)/shard_map/pmax | solution.py:20
  43.5 8.3 %pmax.29 = f32[]{:T(128)} all-reduce(f32[]{:T(128)} %pmax.28), channel_id=1, replica_groups=mesh['row_0'=8,'row_1'=2,'col_0'=8,'col_1'=4] {'row_1'}, use_global_device_ids=true, to_apply=%region_2.3 | all-reduce | flops 1 | bytes 8 | tf_op jit(solution)/shard_map/pmax | solution.py:20
  51.9 13.0 %pmax.30 = f32[]{:T(128)} all-reduce(f32[]{:T(128)} %pmax.29), channel_id=1, replica_groups=mesh['row_0'=8,'row_1'=2,'col_0'=8,'col_1'=4] {'col_0'}, use_global_device_ids=true, to_apply=%region_3.4 | all-reduce | flops 1 | bytes 8 | tf_op jit(solution)/shard_map/pmax | solution.py:20
  64.9 0.9 slice_bitcast_fusion.1
  65.7 0.6 fusion.34
  66.3 7.2 %pmax.31 = f32[]{:T(128)} all-reduce(f32[]{:T(128)} %pmax.30), channel_id=1, replica_groups=mesh['row_0'=8,'row_1'=2,'col_0'=8,'col_1'=4] {'col_1'}, use_global_device_ids=true, to_apply=%region_4.5 | all-reduce | flops 1 | bytes 8 | tf_op jit(solution)/shard_map/pmax | solution.py:20
  73.5 1.3 mul.233
  76.8 2.2 %fusion.12 = f32[1536,528]{0,1:T(8,128)S(1)} fusion(bf16[268,528]{0,1:T(8,128)(2,1)S(1)} %bitcast.99, bf16[2,1536]{1,0:T(2,128)(2,1)S(1)} %collective-permute-done.3, bf16[264,1536]{1,0:T(8,128)(2,1)} %copy-done.4, bf16[2,1536]{1,0:T(2,128)(2,1)S(1)} %collective-permute-done.2), kind=kOutput, calls=%fused_computation.21 | convolution fusion | flops 437170176 | bytes 4350336 | tf_op jit(solution)/shard_map/dot_general | solution.py:114
  79.0 1.7 %copy-done.1 = f32[1536,528]{0,1:T(8,128)} copy-done((f32[1536,528]{0,1:T(8,128)}, f32[1536,528]{0,1:T(8,128)S(1)}, u32[]{:S(2)}) %copy-start.1) | copy-done | bytes 3244056
  80.7 0.8 broadcast_in_dim.67
  81.6 9.8 %all-to-all-start.1 = ((f32[16,2,2,1536]{3,1,2,0:T(2,128)}), f32[16,2,2,1536]{3,1,2,0:T(2,128)}, u32[]{:S(2)}, u32[]{:S(2)}) async-start(f32[16,2,2,1536]{3,1,2,0:T(2,128)} %broadcast_in_dim.67), calls=%async_computation.1 | async-start | bytes 786432 | tf_op jit(solution)/shard_map/all_to_all | solution.py:47
  91.4 0.4 copy.43
  91.8 0.5 copy.44
  92.3 2.7 %fusion.35 = (bf16[3168,256]{1,0:T(8,128)(2,1)S(1)}, f32[3168,256]{1,0:T(8,128)}) fusion(bf16[132,256]{1,0:T(8,128)(2,1)S(1)} %bitcast.108, bf16[3168,2]{1,0:T(8,128)(2,1)S(1)} %copy.44, bf16[3168,128]{1,0:T(8,128)(2,1)S(1)} %bitcast.104, bf16[3168,2]{1,0:T(8,128)(2,1)S(1)} %copy.43), kind=kOutput, calls=%fused_computation.66 | convolution fusion | flops 217426176 | bytes 5769984 | tf_op jit(solution)/shard_map/dot_general | solution.py:87
  95.0 1.6 %slice_reduce_fusion.3 = (bf16[3168]{0:T(1024)(128)(2,1)S(1)}, bf16[3168]{0:T(1024)(128)(2,1)S(1)}, bf16[3168]{0:T(1024)(128)(2,1)S(1)}, bf16[3168]{0:T(1024)(128)(2,1)S(1)}) fusion(bf16[3168,256]{1,0:T(8,128)(2,1)S(1)} %get-tuple-element.30), kind=kLoop, calls=%fused_computation.30 | loop fusion | bytes 50688 | tf_op jit(solution)/shard_map/slice | solution.py:92
  96.9 9.1 %all-to-all-done.1 = f32[16,2,2,1536]{3,1,2,0:T(2,128)} async-done(((f32[16,2,2,1536]{3,1,2,0:T(2,128)}), f32[16,2,2,1536]{3,1,2,0:T(2,128)}, u32[]{:S(2)}, u32[]{:S(2)}) %all-to-all-start.1) | async-done | bytes 393248 | tf_op jit(solution)/shard_map/all_to_all | solution.py:47
  106.0 1.3 broadcast_in_dim.64
  107.4 6.5 %all-to-all-start = ((bf16[32,2,2,3168]{3,1,2,0:T(2,128)(2,1)}), bf16[32,2,2,3168]{3,1,2,0:T(2,128)(2,1)S(1)}, u32[]{:S(2)}, u32[]{:S(2)}) async-start(bf16[32,2,2,3168]{3,1,2,0:T(2,128)(2,1)} %broadcast_in_dim.64), calls=%async_computation | async-start | bytes 1638400 | tf_op jit(solution)/shard_map/all_to_all | solution.py:47
  113.9 1.0 copy.49
  114.9 0.3 reshape.86
  115.2 1.0 convolution_bitcast_fusion.1
  116.3 2.5 %multiply_add_fusion = f32[2,264,1536]{2,1,0:T(8,128)S(1)} fusion(f32[2,264,1536]{2,1,0:T(8,128)} %bitcast.101, f32[2,264]{1,0:T(2,128)S(1)} %get-tuple-element.32, f32[2,1536]{1,0:T(2,128)S(1)} %get-tuple-element.34, f32[2,264]{1,0:T(2,128)S(1)} %get-tuple-element.33, f32[2,1536]{1,0:T(2,128)S(1)} %get-tuple-element.35), kind=kLoop, calls=%fused_computation.3 | loop fusion | flops 3244032 | bytes 6516864 | tf_op jit(solution)/shard_map/add | solution.py:129
  118.8 1.9 %fusion.28 = (f32[1,264,1536]{2,1,0:T(8,128)}, f32[1,264,1536]{2,1,0:T(8,128)}) fusion(f32[2,264,1536]{2,1,0:T(8,128)S(1)} %multiply_add_fusion), kind=kLoop, calls=%fused_computation.59 | loop fusion | bytes 6488064 | tf_op jit(solution)/shard_map/slice | solution.py:133
  120.7 1.8 %reshape_squeeze.13 = f32[264,3,4,128]{3,2,1,0:T(4,128)S(1)} reshape(f32[1,264,1536]{2,1,0:T(8,128)} %get-tuple-element.10) | data formatting | bytes 3244032 | tf_op jit(solution)/shard_map/reshape;squeeze | solution.py:133
  122.6 2.8 %reshape_squeeze.15 = f32[264,3,4,128]{3,2,1,0:T(4,128)} reshape(f32[1,264,1536]{2,1,0:T(8,128)} %get-tuple-element.11) | data formatting | bytes 3244032 | tf_op jit(solution)/shard_map/reshape;squeeze | solution.py:134
  125.3 11.8 %all-to-all-done = bf16[32,2,2,3168]{3,1,2,0:T(2,128)(2,1)S(1)} async-done(((bf16[32,2,2,3168]{3,1,2,0:T(2,128)(2,1)}), bf16[32,2,2,3168]{3,1,2,0:T(2,128)(2,1)S(1)}, u32[]{:S(2)}, u32[]{:S(2)}) %all-to-all-start) | async-done | bytes 811040 | tf_op jit(solution)/shard_map/all_to_all | solution.py:47
  137.1 1.5 copy.46
  138.6 2.3 %reshape.82 = bf16[64,2,3168]{2,0,1:T(8,128)(2,1)S(1)} reshape(bf16[32,2,2,3168]{3,1,0,2:T(2,128)(2,1)} %copy.46) | data formatting | bytes 1622016 | tf_op jit(solution)/shard_map/reshape | solution.py:42
  140.9 1.1 convolution_bitcast_fusion
  142.2 4.8 %fusion = f32[3168,2,128]{2,0,1:T(8,128)S(1)} fusion(f32[2,128]{1,0:T(2,128)S(1)} %bitcast.113, f32[3168,2]{0,1:T(2,128)S(1)} %bitcast.109, f32[2,128]{1,0:T(2,128)S(1)} %bitcast.112, f32[3168,2]{0,1:T(2,128)S(1)} %bitcast.110, f32[3168,256]{1,0:T(8,128)} %get-tuple-element.31), kind=kLoop, calls=%fused_computation.2 | loop fusion | flops 3244032 | bytes 6540800 | tf_op jit(solution)/shard_map/add | solution.py:100
  147.1 0.2 fusion.29
  147.3 1.1 copy-done.3
  148.5 0.3 copy-done.6
  148.8 2.7 %select_convert_fusion = (bf16[3,4,264,128]{3,2,1,0:T(8,128)(2,1)}, bf16[3,4,264,128]{3,2,1,0:T(8,128)(2,1)}) fusion(bf16[3,4,264,128]{3,2,1,0:T(8,128)(2,1)S(1)} %copy-done.6, f32[]{:T(128)S(6)} %div.3, pred[264]{0:T(512)(128)(4,1)S(1)} %copy-done.11, f32[264]{0:T(512)S(1)} %copy-done.14, f32[264,3,4,128]{3,2,1,0:T(4,128)S(1)} %copy-done.3, ...), kind=kLoop, calls=%fused_computation.20 | loop fusion | flops 9732096 | bytes 10007404 | tf_op jit(solution)/shard_map/convert_element_type | solution.py:151
  (63 shorter events, 0.9 us)
Async XLA Ops:
  0.6 76.1 %copy-start = (bf16[268,2,264]{0,2,1:T(8,128)(2,1)S(1)}, bf16[268,2,264]{0,2,1:T(8,128)(2,1)}, u32[]{:S(2)}) copy-start(bf16[268,2,264]{0,2,1:T(8,128)(2,1)} %param.23) | copy-start | bytes 849028
  2.4 10.8 %copy-start.20 = (s32[16]{0:T(128)S(1)}, s32[16]{0:T(128)}, u32[]{:S(2)}) copy-start(s32[16]{0:T(128)} %param.15) | copy-start | bytes 196
  2.4 13.1 %copy-start.2 = (bf16[3,4,264,128]{3,2,1,0:T(8,128)(2,1)S(1)}, bf16[3,4,264,128]{3,2,1,0:T(8,128)(2,1)}, u32[]{:S(2)}) copy-start(bf16[3,4,264,128]{3,2,1,0:T(8,128)(2,1)} %param.13) | copy-start | bytes 2433028
  2.8 88.6 %collective-permute-start = (bf16[3168,2]{0,1:T(2,128)(2,1)S(1)}, bf16[3168,2]{0,1:T(2,128)(2,1)S(1)}, u32[]{:S(2)}, u32[]{:S(2)}) collective-permute-start(bf16[3168,2]{0,1:T(2,128)(2,1)S(1)} %copy.41), channel_id=1, source_target_pairs={{0,1},{1,2},{2,3},{3,4},{4,5},{5,6},{6,7},{7,8},{8,9},{9,10},{10,1... | collective-permute-start | bytes 38024 | tf_op jit(solution)/shard_map/ppermute | solution.py:31
  7.1 84.8 %collective-permute-start.1 = (bf16[3168,2]{0,1:T(2,128)(2,1)S(1)}, bf16[3168,2]{0,1:T(2,128)(2,1)S(1)}, u32[]{:S(2)}, u32[]{:S(2)}) collective-permute-start(bf16[3168,2]{0,1:T(2,128)(2,1)S(1)} %copy.42), channel_id=1, source_target_pairs={{1,0},{2,1},{3,2},{4,3},{5,4},{6,5},{7,6},{8,7},{9,8},{10,9},{11,1... | collective-permute-start | bytes 38024 | tf_op jit(solution)/shard_map/ppermute | solution.py:34
  14.3 8.3 %copy-start.10 = (pred[264]{0:T(512)(128)(4,1)}, pred[264]{0:T(512)(128)(4,1)S(1)}, u32[]{:S(2)}) copy-start(pred[264]{0:T(512)(128)(4,1)S(1)} %iota_compare_fusion) | copy-start | bytes 796
  15.8 6.8 %copy-start.8 = (f32[264]{0:T(512)S(1)}, f32[264]{0:T(512)}, u32[]{:S(2)}) copy-start(f32[264]{0:T(512)} %param.18) | copy-start | bytes 3172
  15.8 6.8 %copy-start.15 = (f32[128]{0:T(128)S(1)}, f32[128]{0:T(128)}, u32[]{:S(2)}) copy-start(f32[128]{0:T(128)} %param.16) | copy-start | bytes 1540
  15.8 27.7 %copy-start.9 = (f32[1,2,2,264]{3,2,1,0:T(2,128)S(1)}, f32[1,2,2,264]{3,2,1,0:T(2,128)}, u32[]{:S(2)}) copy-start(f32[1,2,2,264]{3,2,1,0:T(2,128)} %param.25) | copy-start | bytes 12676
  16.3 0.9 copy-start.4
  17.8 58.9 %collective-permute-start.2 = (bf16[2,1536]{1,0:T(2,128)(2,1)}, bf16[2,1536]{1,0:T(2,128)(2,1)S(1)}, u32[]{:S(2)}, u32[]{:S(2)}) collective-permute-start(bf16[2,1536]{1,0:T(2,128)(2,1)} %get-tuple-element.20), channel_id=1, source_target_pairs={{0,32},{32,64},{64,96},{96,128},{128,160},{160,192},{192,224},{224... | collective-permute-start | bytes 18440 | tf_op jit(solution)/shard_map/ppermute | solution.py:31
  23.5 53.3 %collective-permute-start.3 = (bf16[2,1536]{1,0:T(2,128)(2,1)}, bf16[2,1536]{1,0:T(2,128)(2,1)S(1)}, u32[]{:S(2)}, u32[]{:S(2)}) collective-permute-start(bf16[2,1536]{1,0:T(2,128)(2,1)} %get-tuple-element.21), channel_id=1, source_target_pairs={{32,0},{64,32},{96,64},{128,96},{160,128},{192,160},{224,192},{256... | collective-permute-start | bytes 18440 | tf_op jit(solution)/shard_map/ppermute | solution.py:34
  51.9 13.9 %copy-start.17 = (f32[2,2,128]{2,1,0:T(2,128)S(1)}, f32[2,2,128]{2,1,0:T(2,128)}, u32[]{:S(2)}) copy-start(f32[2,2,128]{2,1,0:T(2,128)} %param.22) | copy-start | bytes 6148
  51.9 23.0 %copy-start.7 = (bf16[132,2,128]{2,1,0:T(2,128)(2,1)S(1)}, bf16[132,2,128]{2,1,0:T(2,128)(2,1)}, u32[]{:S(2)}) copy-start(bf16[132,2,128]{2,1,0:T(2,128)(2,1)} %param.20) | copy-start | bytes 202756
  78.9 1.7 %copy-start.1 = (f32[1536,528]{0,1:T(8,128)}, f32[1536,528]{0,1:T(8,128)S(1)}, u32[]{:S(2)}) copy-start(f32[1536,528]{0,1:T(8,128)S(1)} %fusion.12) | copy-start | bytes 9732100
  81.6 24.5 %all-to-all-start.1 = ((f32[16,2,2,1536]{3,1,2,0:T(2,128)}), f32[16,2,2,1536]{3,1,2,0:T(2,128)}, u32[]{:S(2)}, u32[]{:S(2)}) async-start(f32[16,2,2,1536]{3,1,2,0:T(2,128)} %broadcast_in_dim.67), calls=%async_computation.1 | async-start | bytes 786432 | tf_op jit(solution)/shard_map/all_to_all | solution.py:47
  107.4 29.8 %all-to-all-start = ((bf16[32,2,2,3168]{3,1,2,0:T(2,128)(2,1)}), bf16[32,2,2,3168]{3,1,2,0:T(2,128)(2,1)S(1)}, u32[]{:S(2)}, u32[]{:S(2)}) async-start(bf16[32,2,2,3168]{3,1,2,0:T(2,128)(2,1)} %broadcast_in_dim.64), calls=%async_computation | async-start | bytes 1638400 | tf_op jit(solution)/shard_map/all_to_all | solution.py:47
  138.6 3.6 %copy-start.12 = (f32[2,1,128]{2,1,0:T(1,128)S(1)}, f32[2,1,128]{2,1,0:T(1,128)}, u32[]{:S(2)}) copy-start(f32[2,1,128]{2,1,0:T(1,128)} %get-tuple-element.28) | copy-start | bytes 3076
  138.6 3.6 %copy-start.13 = (f32[2,1,128]{2,1,0:T(1,128)S(1)}, f32[2,1,128]{2,1,0:T(1,128)}, u32[]{:S(2)}) copy-start(f32[2,1,128]{2,1,0:T(1,128)} %get-tuple-element.29) | copy-start | bytes 3076
  147.0 1.4 copy-start.3
  147.0 1.5 %copy-start.5 = (f32[4,264,128]{2,1,0:T(8,128)S(1)}, f32[4,264,128]{2,1,0:T(8,128)}, u32[]{:S(2)}) copy-start(f32[4,264,128]{2,1,0:T(8,128)} %get-tuple-element.17) | copy-start | bytes 1622020
  147.0 1.8 %copy-start.6 = (bf16[3,4,264,128]{3,2,1,0:T(8,128)(2,1)S(1)}, bf16[3,4,264,128]{3,2,1,0:T(8,128)(2,1)}, u32[]{:S(2)}) copy-start(bf16[3,4,264,128]{3,2,1,0:T(8,128)(2,1)} %param.14) | copy-start | bytes 2433028
  147.0 1.8 %copy-start.11 = (pred[264]{0:T(512)(128)(4,1)S(1)}, pred[264]{0:T(512)(128)(4,1)}, u32[]{:S(2)}) copy-start(pred[264]{0:T(512)(128)(4,1)} %copy-done.10) | copy-start | bytes 796
  147.0 1.8 %copy-start.14 = (f32[264]{0:T(512)S(1)}, f32[264]{0:T(512)}, u32[]{:S(2)}) copy-start(f32[264]{0:T(512)} %param.19) | copy-start | bytes 3172
  147.0 1.7 %copy-start.16 = (f32[128]{0:T(128)S(1)}, f32[128]{0:T(128)}, u32[]{:S(2)}) copy-start(f32[128]{0:T(128)} %param.16) | copy-start | bytes 1540
  147.1 1.7 %copy-start.18 = (f32[128]{0:T(128)S(1)}, f32[128]{0:T(128)}, u32[]{:S(2)}) copy-start(f32[128]{0:T(128)} %param.17) | copy-start | bytes 1540
  147.1 1.7 %copy-start.19 = (f32[128]{0:T(128)S(1)}, f32[128]{0:T(128)}, u32[]{:S(2)}) copy-start(f32[128]{0:T(128)} %mul.233) | copy-start | bytes 1540
where the time goes:
time: 153 us; the launch traced here: 152 us
  blocking collectives  44.1 us (29%)
  starting transfers between devices  35.6 us (23%)
  local copies, waits for them, and re-layouts  26.7 us (17%)
  waiting for transfers between devices  20.9 us (14%)
  other arithmetic  13.1 us (9%)
  matrix products  7.07 us (5%)
  between operations  4.08 us (3%)
    pmax x4, blocking collectives, by_axis(): value = lax.pmax(value, axis)  44.1 us
    all_to_all x2, waiting for transfers between devices, copy_for_each(): lax.all_to_all(jnp.broadcast_to(value[None], (length, *value.shape)), axi...  20.9 us
    all_to_all x2, starting transfers between devices, copy_for_each(): lax.all_to_all(jnp.broadcast_to(value[None], (length, *value.shape)), axi...  16.3 us
    ppermute x2, starting transfers between devices, padded_2(): lax.ppermute(lax.slice_in_dim(block, 0, width, axis=dim), axis, backward)  10.4 us
    ppermute x2, starting transfers between devices, padded_2(): lax.ppermute(lax.slice_in_dim(block, block.shape[dim] - width, None, axis...  8.78 us
    add x1, other arithmetic, shards(): local_x.reshape(line_count, 2, x_width)  4.77 us
    unnamed x48, local copies, waits for them, and re-layouts  4.28 us
  transfers between devices with their start and end apart: 6, of which 2 were waited for; matrix products, arithmetic and copies ran while one was open for 18% of the time, Pallas kernels for 0%

commit v1 on v0

v1 whole, which is shorter than its diff:
```python
import jax
import jax.numpy as jnp
from jax import lax
from jax.experimental import pallas as pl
from jax.experimental.pallas import tpu as pltpu
from jax.sharding import Mesh
from jax.sharding import PartitionSpec as P

COL = ("col_0", "col_1")
ROW = ("row_0", "row_1")

viscosity = 0.1
cfl_target = 1.5
gamma_coef = 5.0 / 12.0
zeta_coef = -17.0 / 60.0

F32 = jnp.float32
BF16 = jnp.bfloat16
NCOL = 32
NROW = 16
XW = 128
YR = 264
NP = 12
LINES = NP * YR
CHUNK = 112
CHUNKS = -(-LINES // CHUNK)
HALF = NP // 2
TILES = HALF + 1
EDGE_X = (0, 1, XW - 2, XW - 1)
HALO_X = (0, 1, XW + 2, XW + 3)


def nn(a, b, precision=None):
    return lax.dot_general(
        a, b, (((1,), (0,)), ((), ())), precision=precision, preferred_element_type=F32
    )


def nt(a, b):
    return lax.dot_general(a, b, (((1,), (1,)), ((), ())), preferred_element_type=F32)


def tn(a, b):
    return lax.dot_general(a, b, (((0,), (0,)), ((), ())), preferred_element_type=F32)


def iota(shape, dim):
    return lax.broadcasted_iota(jnp.int32, shape, dim)


def ones_where(cond):
    return jnp.where(cond, F32(1.0), F32(0.0))


def row_pos():
    return lax.axis_index("row_0") * 2 + lax.axis_index("row_1")


def three_parts(value):
    high = value.astype(BF16).astype(F32)
    rest = value - high
    mid = rest.astype(BF16).astype(F32)
    return high, mid, rest - mid


def max_tile(value):
    high, mid, low = three_parts(jnp.broadcast_to(value, (8, 128)))
    row = iota((8, 128), 0)
    return jnp.where(
        row == 0, high, jnp.where(row == 1, mid, jnp.where(row == 2, low, F32(0.0)))
    )


def column_tiles(row_ref, row):
    pieces = []
    for j in range(3):
        seg = row_ref[row : row + 1, 128 * j : 128 * j + 128]
        pieces.append(jnp.transpose(jnp.broadcast_to(seg, (128, 128))))
    return jnp.concatenate([pieces[0], pieces[1], pieces[2][0 : YR - 256]], axis=0)


def x_partial_kernel(v_ref, x_ref, o_ref):
    row, lane = iota((8, XW), 0), iota((8, XW), 1)
    pick = ones_where((row < 4) & (lane == (XW - 1) * (row % 2))).astype(BF16)
    ends = nt(pick, x_ref[...])
    row_e = iota((8, 2 * (XW + 4)), 0)
    weights = jnp.where(row == 4, ones_where(lane == EDGE_X[0]), F32(0.0))
    for j in range(1, 4):
        weights = jnp.where(row == 4 + j, ones_where(lane == EDGE_X[j]), weights)
    src, dst = iota((2 * (XW + 4), XW), 0), iota((2 * (XW + 4), XW), 1)
    for k in range(2):
        spread = ones_where(src == 2 * (dst + 2) + k).astype(BF16)
        mine = jnp.where((row_e // 2) == k, ends, F32(0.0)).astype(BF16)
        weights = weights + nn(mine, spread)
    weights = weights.astype(BF16)
    for d in range(NCOL):
        first = CHUNK * d
        if first + 128 <= LINES:
            o_ref[d] = nt(weights, v_ref[first : first + 128, :]).astype(BF16)
        elif first < LINES:
            part = nt(weights, v_ref[first:LINES, :])
            rest = jnp.zeros((8, 128 - (LINES - first)), F32)
            o_ref[d] = jnp.concatenate([part, rest], axis=1).astype(BF16)
        else:
            o_ref[d] = jnp.zeros((8, 128), BF16)


def y_partial_kernel(count_ref, v_ref, w_ref, xs_ref, ys_ref, o_ref, pad_ref):
    count = count_ref[row_pos()]
    row, slot = iota((8, YR), 0), iota((8, YR), 1)
    place = jnp.where(row % 2 == 0, 0, count - 1)
    ends = nn(ones_where((row < 2) & (slot == place)).astype(BF16), w_ref[0])
    ends = ends + nn(
        ones_where((row >= 2) & (row < 4) & (slot == place)).astype(BF16), w_ref[1]
    )
    pad_ref[...] = jnp.zeros_like(pad_ref)
    pad_ref[0:8, 0 : YR + 4] = ends
    pad_ref[8:9, 0:YR] = ys_ref[...]
    wide = pad_ref[0:8, :]
    own = pltpu.roll(wide, 384 - 2, 1)[:, 0:YR]
    edge = jnp.where(
        row == 4, 0, jnp.where(row == 5, 1, jnp.where(row == 6, count - 2, count - 1))
    )
    weights = jnp.where(
        row < 4, jnp.where(slot < count, own, F32(0.0)), ones_where(slot == edge)
    ).astype(BF16)
    lane8, row8 = iota((8, 128), 1), iota((8, 128), 0)
    margin = jnp.where(
        lane8 < 2, wide[:, 0:128], pltpu.roll(wide[:, 256:384], 128 - (YR - 256), 1)
    )
    ys = column_tiles(pad_ref, 8)
    live = iota((YR, XW), 0) < count
    top = jnp.zeros((YR, XW), F32)
    for z in range(4):
        speed = jnp.abs(v_ref[z].astype(F32)) * xs_ref[...]
        speed = speed + jnp.abs(v_ref[4 + z].astype(F32)) * ys
        top = jnp.maximum(top, speed)
    top = jnp.where(live, top, F32(0.0))
    top = jnp.max(jnp.max(top, axis=0, keepdims=True), axis=1, keepdims=True)
    last = jnp.where(row8 < 4, margin, pltpu.roll(max_tile(top), 4, 0))
    for half in range(2):
        tiles = [nn(weights, v_ref[HALF * half + g]) for g in range(HALF)]
        whole = jnp.concatenate(tiles + [last], axis=0).astype(BF16)
        for chip in range(NROW // 2):
            o_ref[2 * chip + half] = whole


def x_solve_kernel(c_ref, x_ref, coupling_ref, o_ref, a_ref, e_ref, s_ref):
    a_ref[...] = c_ref[...].astype(F32).reshape(NCOL * 8, 128)
    part = [a_ref[pl.ds(v, NCOL, stride=8), :] for v in range(8)]
    margin = [pltpu.roll(part[6], 1, 0), pltpu.roll(part[7], 1, 0)]
    margin += [pltpu.roll(part[4], NCOL - 1, 0), pltpu.roll(part[5], NCOL - 1, 0)]
    local = x_ref[...].astype(F32)
    for k in range(2):
        for e in range(2):
            ends = part[2 * k + e]
            lane = (XW - 1) * e
            for h in range(4):
                place = 2 * HALO_X[h] + k
                ends = ends + local[place : place + 1, lane : lane + 1] * margin[h]
            e_ref[k, pl.ds(e, NCOL, stride=2), :] = ends
        s_ref[k] = nn(coupling_ref[k], e_ref[k], lax.Precision.HIGHEST)
        for e in range(2):
            a_ref[pl.ds(2 * k + e, NCOL, stride=8), :] = s_ref[k, pl.ds(e, NCOL, stride=2), :]
    for h in range(4):
        a_ref[pl.ds(4 + h, NCOL, stride=8), :] = margin[h]
    o_ref[...] = a_ref[...].reshape(NCOL, 8, 128).astype(BF16)


def top_kernel(s_ref, r_ref, o_ref):
    last = r_ref[...][:, 8 * HALF : 8 * TILES, :].astype(F32)
    row = iota((NROW, 8, 128), 1)
    parts = jnp.where((row >= 4) & (row < 7), last, F32(0.0))
    top = jnp.max(jnp.sum(parts, axis=1), axis=0, keepdims=True)
    spare = iota((8, 128), 1) >= CHUNK
    tile = max_tile(top)
    o_ref[...] = jnp.where(spare[None], tile[None], s_ref[...].astype(F32)).astype(BF16)


def y_solve_kernel(r_ref, coupling_ref, keep_ref, send_ref, a_ref, e_ref, s_ref, m_ref):
    a_ref[...] = r_ref[...].astype(F32).reshape(NROW * 8 * TILES, 128)

    def rows_of(place):
        return a_ref[pl.ds(place, NROW, stride=8 * TILES), :]

    source = iota((NROW, 128), 0)
    weights = [rows_of(8 * HALF + j) for j in range(4)]
    weight = [
        [jnp.broadcast_to(weights[j][:, h : h + 1], (NROW, 128)) for h in range(4)]
        for j in range(4)
    ]
    for g in range(HALF):
        lanes = slice(128 * g, 128 * g + 128)
        part = [rows_of(8 * g + v) for v in range(8)]
        margin = [pltpu.roll(part[6 + h], 1, 0) for h in range(2)]
        margin = [jnp.where(source == 0, F32(0.0), m) for m in margin]
        upper = [pltpu.roll(part[4 + h], NROW - 1, 0) for h in range(2)]
        margin += [jnp.where(source == NROW - 1, F32(0.0), m) for m in upper]
        for h in range(4):
            m_ref[h, :, lanes] = margin[h]
        for k in range(2):
            for e in range(2):
                ends = part[2 * k + e]
                for h in range(4):
                    ends = ends + weight[2 * k + e][h] * margin[h]
                e_ref[HALF * k + g, pl.ds(e, NROW, stride=2), :] = ends
    for k in range(2):
        ends = jnp.concatenate([e_ref[HALF * k + g] for g in range(HALF)], axis=1)
        s_ref[k] = nn(coupling_ref[k], ends, lax.Precision.HIGHEST)
    core = lax.axis_index("row_1")
    own = row_pos()
    for block, out in ((own, keep_ref), (own + 1 - 2 * core, send_ref)):
        pieces = [s_ref[k, pl.ds(2 * block + e, 1), :] for k in range(2) for e in range(2)]
        pieces += [m_ref[h, pl.ds(block, 1), :] for h in range(4)]
        out[...] = jnp.concatenate(pieces, axis=0).astype(BF16)


def prepare_kernel(
    count_ref, x_ref, xb_ref, w_ref, yb_ref, ys_ref, yc_ref,
    xo_ref, xc_ref, wm_ref, hc_ref, yy_ref, pad_ref,
):
    count = count_ref[row_pos()]
    x_all = x_ref[...]
    n_in = 2 * (XW + 4)
    dst, src = iota((XW, n_in), 0), iota((XW, n_in), 1)
    row, col = iota((8, n_in), 0), iota((8, n_in), 1)
    row_x, row_y = iota((8, XW), 0), iota((8, YR), 0)
    row_h, col_h = iota((8, YR + 4), 0), iota((8, YR + 4), 1)
    slot_in, slot_out = iota((YR + 4, YR), 0), iota((YR + 4, YR), 1)
    shift = ones_where((slot_in == slot_out + 2) & (slot_out < count)).astype(BF16)

    def placed(values, offsets):
        found = jnp.where(values[0] == 4, offsets[0], -1)
        for h in range(1, 4):
            found = jnp.where(values[0] == 4 + h, offsets[h], found)
        return ones_where(values[1] == found).astype(BF16)

    x_high = xb_ref[...].astype(BF16).astype(F32)
    y_high = yb_ref[...].astype(BF16).astype(F32)
    pick_y = placed((row_h, col_h), (0, 1, YR + 2, YR + 3))
    for k in range(2):
        lanes = slice(XW * k, XW * k + XW)
        xo_ref[:, lanes] = nn(ones_where(src == 2 * (dst + 2) + k).astype(BF16), x_all).astype(BF16)
        pick_x = placed((row, col), [2 * h + k for h in HALO_X])
        mine = (row_x // 2) == k
        head = jnp.where(mine, x_high, F32(0.0)) + nn(pick_x, x_all)
        tail = jnp.where(mine, xb_ref[...] - x_high, F32(0.0))
        xc_ref[:, lanes] = jnp.concatenate([head, tail], axis=0).astype(BF16)
        wm_ref[k] = nn(w_ref[k], shift).astype(BF16)
        mine = (row_y // 2) == k
        head = jnp.where(mine, y_high, F32(0.0)) + nt(pick_y, w_ref[k])
        tail = jnp.where(mine, yb_ref[...] - y_high, F32(0.0))
        hc_ref[k] = jnp.concatenate([head, tail], axis=0).astype(BF16)
    pad_ref[...] = jnp.zeros_like(pad_ref)
    pad_ref[0:1, 0:YR] = ys_ref[...]
    pad_ref[1:2, 0:YR] = yc_ref[...]
    scale = column_tiles(pad_ref, 0)
    yy_ref[0] = scale
    yy_ref[1] = viscosity * column_tiles(pad_ref, 1)
    yy_ref[2] = viscosity * scale * scale


def finish_kernel(
    count_ref, c_ref, keep_ref, got_ref, v_ref, p_ref, xs_ref, xv_ref,
    xo_ref, xc_ref, wm_ref, hc_ref, yy_ref, rhs_ref, inc_ref, x_add,
):
    count = count_ref[row_pos()]
    core = lax.axis_index("row_1")
    row, lane = iota((NCOL, 8, 128), 1), iota((NCOL, 8, 128), 2)
    tops = jnp.where((lane >= CHUNK) & (row < 3), c_ref[...].astype(F32), F32(0.0))
    top = jnp.max(jnp.sum(tops, axis=1), axis=0, keepdims=True)
    step = cfl_target / (jnp.max(top, axis=1, keepdims=True) + 1e-06)
    x_corr = xc_ref[...]
    for d in range(CHUNKS):
        coef = c_ref[d].astype(F32)
        coef = jnp.concatenate([coef, coef], axis=0).astype(BF16)
        x_add[CHUNK * d : CHUNK * d + 128, :] = tn(coef, x_corr)
    live = iota((YR, XW), 0) < count
    xs, xv = xs_ref[...], viscosity * xv_ref[...]
    x_second = viscosity * xs * xs
    for pair in range(2):
        for f in range(3):
            plane = 4 * f + 2 * pair
            half, g = divmod(plane, HALF)
            lanes = slice(128 * g, 128 * g + 256)
            coef = jnp.where(core == half, keep_ref[:, lanes].astype(F32), got_ref[:, lanes].astype(F32))
            coef = jnp.concatenate([coef, coef], axis=0).astype(BF16)
            both = jnp.concatenate([v_ref[plane], v_ref[plane + 1]], axis=1)
            y_first = nn(wm_ref[0], both) + tn(hc_ref[0], coef)
            y_second = nn(wm_ref[1], both) + tn(hc_ref[1], coef)
            for j in range(2):
                p, z = plane + j, 2 * pair + j
                at = slice(128 * j, 128 * j + 128)
                in_x = nn(v_ref[p], xo_ref[...]) + x_add[YR * p : YR * p + YR, :]
                u, v = v_ref[z].astype(F32), v_ref[4 + z].astype(F32)
                rhs = (xv - u * xs) * in_x[:, 0:XW] + x_second * in_x[:, XW:]
                rhs = rhs + (yy_ref[1] - v * yy_ref[0]) * y_first[:, at] + yy_ref[2] * y_second[:, at]
                rhs = jnp.where(live, rhs, F32(0.0))
                inc = step * (gamma_coef * rhs + zeta_coef * p_ref[p].astype(F32))
                inc = jnp.where(live, inc, F32(0.0))
                rhs_ref[p] = rhs.astype(BF16)
                inc_ref[p] = inc.astype(BF16)


VMEM = pl.BlockSpec(memory_space=pltpu.VMEM)
SMEM = pl.BlockSpec(memory_space=pltpu.SMEM)


def call(body, name, operands, outs, scratch=(), flops=0, mib=16):
    specs = [SMEM if operand.dtype == jnp.int32 else VMEM for operand in operands]
    size = sum(o.size * o.dtype.itemsize for o in (*operands, *outs))
    single = len(outs) == 1
    return pl.pallas_call(
        body,
        out_shape=outs[0] if single else outs,
        in_specs=specs,
        out_specs=VMEM if single else [VMEM] * len(outs),
        scratch_shapes=[pltpu.VMEM(shape, F32) for shape in scratch],
        compiler_params=pltpu.CompilerParams(vmem_limit_bytes=mib * 2**20),
        cost_estimate=pl.CostEstimate(flops=flops, bytes_accessed=size, transcendentals=0),
        name=name,
    )(*operands)


def shape(dims, kind=BF16):
    return jax.ShapeDtypeStruct(dims, kind)


def shards(
    velocity, rhs_prev, row_counts, x_scale, x_curv, y_scale, y_curv,
    x_local, x_coupling, x_basis, y_local, y_coupling, y_basis,
):
    lines = velocity.reshape(LINES, XW)
    planes = velocity.reshape(NP, YR, XW)
    previous = rhs_prev.reshape(NP, YR, XW)
    x_rows = x_local.reshape(2 * (XW + 4), XW)
    y_mats = jnp.transpose(y_local, (1, 2, 0))
    x_scale, x_curv = x_scale.reshape(1, XW), x_curv.reshape(1, XW)
    y_scale, y_curv = y_scale.reshape(1, YR), y_curv.reshape(1, YR)

    mine = call(x_partial_kernel, "x_partial", (lines, x_rows), (shape((NCOL, 8, 128)),), flops=10**8)
    theirs = lax.all_to_all(mine, COL, 0, 0, tiled=True)
    y_part = call(
        y_partial_kernel, "y_partial", (row_counts, planes, y_mats, x_scale, y_scale),
        (shape((NROW, 8 * TILES, 128)),), ((16, 384),), flops=10**8,
    )
    x_basis = jnp.pad(x_basis.reshape(4, XW), ((0, 4), (0, 0)))
    y_basis = jnp.pad(y_basis.reshape(4, YR), ((0, 4), (0, 0)))
    prepared = call(
        prepare_kernel, "prepare",
        (row_counts, x_rows, x_basis, y_mats, y_basis, y_scale, y_curv),
        (
            shape((XW, 2 * XW)), shape((16, 2 * XW)), shape((2, YR, YR)),
            shape((2, 16, YR)), shape((3, YR, XW), F32),
        ),
        ((8, 384),), flops=10**8,
    )
    columns = lax.all_to_all(y_part, ROW, 0, 0, tiled=True)
    x_solved = call(
        x_solve_kernel, "x_solve", (theirs, x_rows, x_coupling), (shape((NCOL, 8, 128)),),
        ((NCOL * 8, 128), (2, 2 * NCOL, 128), (2, 2 * NCOL, 128)), flops=10**8,
    )
    x_back = call(top_kernel, "top", (x_solved, columns), (shape((NCOL, 8, 128)),))
    x_back = lax.all_to_all(x_back, COL, 0, 0, tiled=True)
    wide = 128 * HALF
    keep, send = call(
        y_solve_kernel, "y_solve", (columns, y_coupling), (shape((8, wide)), shape((8, wide))),
        (
            (NROW * 8 * TILES, 128), (NP, 2 * NROW, 128), (2, 2 * NROW, wide), (4, NROW, wide),
        ), flops=10**8,
    )
    got = lax.ppermute(send, "row_1", [(0, 1), (1, 0)])
    rhs, inc = call(
        finish_kernel, "finish",
        (row_counts, x_back, keep, got, planes, previous, x_scale, x_curv, *prepared),
        (shape((NP, YR, XW)), shape((NP, YR, XW))),
        ((CHUNK * (CHUNKS - 1) + 128, 2 * XW),), flops=6 * 10**8, mib=32,
    )
    return rhs.reshape(velocity.shape), inc.reshape(velocity.shape)


def solution(mesh):
    torus = Mesh(mesh.devices.reshape(8, 2, 8, 4), ("row_0", "row_1", "col_0", "col_1"))
    placed = (
        P(None, None, ROW, COL), P(None, None, ROW, COL), P(), P(COL), P(COL), P(ROW), P(ROW),
        P(), P(), P(), P(ROW, None, None), P(), P(ROW, None, None, None),
    )
    return jax.shard_map(
        shards,
        mesh=torus,
        in_specs=placed,
        out_specs=(P(None, None, ROW, COL), P(None, None, ROW, COL)),
        check_vma=False,
    )
```

time: 153 us -> 67.4 us (0.44)
  blocking collectives: 44.1 us -> 0 us
  local copies, waits for them, and re-layouts: 26.7 us -> 4.4 us
  other arithmetic: 13.1 us -> 0 us
  Pallas kernels: 0 us -> 10.6 us
  matrix products: 7.07 us -> 0 us
  starting transfers between devices: 35.6 us -> 28.8 us
  between operations: 4.08 us -> 0.86 us
    pmax x4 -> x0, blocking collectives: 44.1 us -> none  [by_axis(): value = lax.pmax(value, axis)]
    ppermute x4 -> x1, starting transfers between devices: 19.2 us -> 1.92 us  [shards(): got = lax.ppermute(send, 'row_1', [(0, 1), (1, 0)])]
    pallas_call x0 -> x7, Pallas kernels: none -> 10.6 us  [call(): pl.pallas_call(body, out_shape=outs[0] if single else outs, in_specs=spec...]
    all_to_all x2 -> x3, starting transfers between devices: 16.3 us -> 26.9 us  [the longest x1 12.4 us: shards(): columns = lax.all_to_all(y_part, ROW, 0, 0, tiled=True)]
    add x2 -> x0, other arithmetic: 7.29 us -> none  [the longest x1 4.77 us: shards(): local_x.reshape(line_count, 2, x_width)]
    dot_general x4 -> x0, matrix products: 7.07 us -> none  [the longest x1 2.71 us: shards(): jnp.dot(padded, x_local.reshape(x_width + 4, 2 * x_width), preferred_elem...]
    slice x10 -> x0, local copies, waits for them, and re-layouts: 6.84 us -> none  [the longest x2 2.09 us: padded_2(): lax.slice_in_dim(block, block.shape[dim] - width, None, axis=dim)]
    another operation x8 -> x0, local copies, waits for them, and re-layouts: 4.71 us -> none  [the longest x1 2.8 us: shards(): result_y[1].reshape(y_rows, n_comp, n_plane, x_width)]
  transfers between devices with their start and end apart: 6 -> 4, of which waited for: 2 -> 3; matrix products, arithmetic and copies ran while one was open for 18% -> 0% of each run, Pallas kernels for 0% -> 5%
where the time goes in v1:
time: 67.4 us; the launch traced here: 66.9 us
  starting transfers between devices  28.8 us (43%)
  waiting for transfers between devices  22.1 us (33%)
  Pallas kernels  10.6 us (16%)
  local copies, waits for them, and re-layouts  4.4 us (7%)
  between operations  0.86 us (1%)
    all_to_all x1, starting transfers between devices, shards(): columns = lax.all_to_all(y_part, ROW, 0, 0, tiled=True)  12.4 us
    pallas_call x7, Pallas kernels, call(): pl.pallas_call(body, out_shape=outs[0] if single else outs, in_specs=spec...  10.6 us
    all_to_all x1, starting transfers between devices, shards(): theirs = lax.all_to_all(mine, COL, 0, 0, tiled=True)  10.6 us
    all_to_all x1, waiting for transfers between devices, shards(): columns = lax.all_to_all(y_part, ROW, 0, 0, tiled=True)  10.6 us
    all_to_all x1, waiting for transfers between devices, shards(): x_back = lax.all_to_all(x_back, COL, 0, 0, tiled=True)  6.14 us
    all_to_all x1, waiting for transfers between devices, shards(): theirs = lax.all_to_all(mine, COL, 0, 0, tiled=True)  5.38 us
    unnamed x32, local copies, waits for them, and re-layouts  4.37 us
    all_to_all x1, starting transfers between devices, shards(): x_back = lax.all_to_all(x_back, COL, 0, 0, tiled=True)  3.86 us
  transfers between devices with their start and end apart: 4, of which 3 were waited for; matrix products, arithmetic and copies ran while one was open for 0% of the time, Pallas kernels for 5%

profile of v1, /device:TPU:1, one launch (start us, length us, event | category | flops | bytes accessed | tf_op | source)
XLA Modules:
  0.0 66.9 jit_solution(13765008341901948800)
XLA Ops:
  0.6 0.0 copy-start
  0.6 1.1 %copy-done = bf16[3,4,264,128]{3,2,1,0:T(8,128)(2,1)S(1)} copy-done((bf16[3,4,264,128]{3,2,1,0:T(8,128)(2,1)S(1)}, bf16[3,4,264,128]{3,2,1,0:T(8,128)(2,1)}, u32[]{:S(2)}) %copy-start) | copy-done | bytes 811032
  1.8 0.0 copy-start.5
  1.8 0.9 %copy-done.5 = bf16[132,2,128]{2,1,0:T(2,128)(2,1)S(1)} copy-done((bf16[132,2,128]{2,1,0:T(2,128)(2,1)S(1)}, bf16[132,2,128]{2,1,0:T(2,128)(2,1)}, u32[]{:S(2)}) %copy-start.5) | copy-done | bytes 67608
  2.7 0.0 copy-start.1
  2.7 1.5 %x_partial.1 = bf16[32,8,128]{2,1,0:T(8,128)(2,1)} custom-call(bf16[3168,128]{1,0:T(8,128)(2,1)S(1)} %bitcast.10, bf16[264,128]{1,0:T(8,128)(2,1)S(1)} %bitcast.16), custom_call_target="tpu_custom_call" | custom-call | flops 100000000 | bytes 944128 | tf_op jit(solution)/shard_map/x_partial/pallas_call | solution.py:313
  4.1 0.0 copy-start.13
  4.1 10.6 %all-to-all-start = ((bf16[32,8,128]{2,1,0:T(8,128)(2,1)}), bf16[32,8,128]{2,1,0:T(8,128)(2,1)S(1)}, u32[]{:S(2)}, u32[]{:S(2)}) async-start(bf16[32,8,128]{2,1,0:T(8,128)(2,1)} %x_partial.1), calls=%async_computation | async-start | bytes 131072 | tf_op jit(solution)/shard_map/all_to_all | solution.py:342
  14.8 0.0 copy-done.13
  14.8 0.0 copy-start.7
  14.8 0.0 copy-start.8
  14.8 0.0 copy-done.1
  14.8 0.6 copy-done.7
  15.5 0.0 copy-done.8
  15.5 0.0 copy-start.2
  15.5 1.0 %copy-done.2 = bf16[268,2,264]{0,2,1:T(8,128)(2,1)S(1)} copy-done((bf16[268,2,264]{0,2,1:T(8,128)(2,1)S(1)}, bf16[268,2,264]{0,2,1:T(8,128)(2,1)}, u32[]{:S(2)}) %copy-start.2) | copy-done | bytes 283032
  16.5 1.7 %y_partial.1 = bf16[16,56,128]{2,1,0:T(8,128)(2,1)} custom-call(s32[16]{0:T(128)S(1)} %copy-done.7, bf16[12,264,128]{2,1,0:T(8,128)(2,1)S(1)} %bitcast.11, bf16[2,264,268]{2,1,0:T(8,128)(2,1)S(1)} %bitcast.13, f32[1,128]{1,0:T(1,128)S(1)} %bitcast.19, f32[1,264]{1,0:T(1,128)S(1)} %reshape.44.ys_ref), custom_call_target="tpu_custom_call" | custom-call | flops 100000000 | bytes 1325024 | tf_op jit(solution)/shard_map/y_partial/pallas_call | solution.py:313
  18.2 0.0 copy-start.6
  18.2 0.0 copy-start.10
  18.2 5.4 %all-to-all-done.c_ref = bf16[32,8,128]{2,1,0:T(8,128)(2,1)S(1)} async-done(((bf16[32,8,128]{2,1,0:T(8,128)(2,1)}), bf16[32,8,128]{2,1,0:T(8,128)(2,1)S(1)}, u32[]{:S(2)}, u32[]{:S(2)}) %all-to-all-start) | async-done | bytes 65568 | tf_op jit(solution)/shard_map/all_to_all | solution.py:342
  23.6 12.4 %all-to-all-start.1 = ((bf16[16,56,128]{2,1,0:T(8,128)(2,1)}), bf16[16,56,128]{2,1,0:T(8,128)(2,1)S(1)}, u32[]{:S(2)}, u32[]{:S(2)}) async-start(bf16[16,56,128]{2,1,0:T(8,128)(2,1)} %y_partial.1), calls=%async_computation.1 | async-start | bytes 458752 | tf_op jit(solution)/shard_map/all_to_all | solution.py:358
  36.0 0.0 copy-done.6
  36.0 0.0 copy-done.10
  36.1 0.0 copy-start.11
  36.1 0.0 copy-start.14
  36.1 0.0 copy-start.12
  36.1 0.0 copy-start.15
  36.1 0.0 copy-start.4
  36.1 0.3 x_solve.1.s_ref
  36.5 0.0 copy-start.3
  36.5 10.6 %all-to-all-done.1.r_ref = bf16[16,56,128]{2,1,0:T(8,128)(2,1)S(1)} async-done(((bf16[16,56,128]{2,1,0:T(8,128)(2,1)}), bf16[16,56,128]{2,1,0:T(8,128)(2,1)S(1)}, u32[]{:S(2)}, u32[]{:S(2)}) %all-to-all-start.1) | async-done | bytes 229408 | tf_op jit(solution)/shard_map/all_to_all | solution.py:358
  47.1 0.7 %top.1 = bf16[32,8,128]{2,1,0:T(8,128)(2,1)} custom-call(bf16[32,8,128]{2,1,0:T(8,128)(2,1)S(1)} %x_solve.1.s_ref, bf16[16,56,128]{2,1,0:T(8,128)(2,1)S(1)} %all-to-all-done.1.r_ref), custom_call_target="tpu_custom_call" | custom-call | bytes 360448 | tf_op jit(solution)/shard_map/top/pallas_call | solution.py:313
  47.8 3.9 %all-to-all-start.2 = ((bf16[32,8,128]{2,1,0:T(8,128)(2,1)}), bf16[32,8,128]{2,1,0:T(8,128)(2,1)S(1)}, u32[]{:S(2)}, u32[]{:S(2)}) async-start(bf16[32,8,128]{2,1,0:T(8,128)(2,1)} %top.1), calls=%async_computation.2 | async-start | bytes 131072 | tf_op jit(solution)/shard_map/all_to_all | solution.py:364
  51.6 0.0 copy-done.11
  51.6 0.5 y_solve.1
  52.1 1.9 %collective-permute-start = (bf16[8,768]{1,0:T(8,128)(2,1)S(1)}, bf16[8,768]{1,0:T(8,128)(2,1)S(1)}, u32[]{:S(2)}, u32[]{:S(2)}) collective-permute-start(bf16[8,768]{1,0:T(8,128)(2,1)S(1)} %get-tuple-element.12), channel_id=1, source_target_pairs={{0,32},{32,0},{1,33},{33,1},{2,34},{34,2},{3,35},{35,3},{4,36},{36... | collective-permute-start | bytes 36872 | tf_op jit(solution)/shard_map/ppermute | solution.py:372
  54.0 0.0 copy-done.14
  54.0 0.0 copy-done.12
  54.1 0.0 copy-done.15
  54.1 0.0 copy-done.3
  54.1 1.1 %prepare.1 = (bf16[128,256]{1,0:T(8,128)(2,1)S(1)}, bf16[16,256]{1,0:T(8,128)(2,1)S(1)}, bf16[2,264,264]{2,1,0:T(8,128)(2,1)S(1)}, bf16[2,16,264]{2,1,0:T(8,128)(2,1)S(1)}, f32[3,264,128]{2,1,0:T(8,128)S(1)}) custom-call(s32[16]{0:T(128)S(1)} %copy-done.7, bf16[264,128]{1,0:T(8,128)(2,1)S(1)} %bitcast.18, f32[8,128]{1,0:T(8,128)S(1)} %pad.8.xb_ref, ...), custom_call_target="tpu_custom_call" | custom-call | flops 100000000 | bytes 1140224 | tf_op jit(solution)/shard_map/prepare/pallas_call | solution.py:313
  55.2 0.0 collective-permute-done.got_ref
  55.2 6.1 %all-to-all-done.2.c_ref = bf16[32,8,128]{2,1,0:T(8,128)(2,1)S(1)} async-done(((bf16[32,8,128]{2,1,0:T(8,128)(2,1)}), bf16[32,8,128]{2,1,0:T(8,128)(2,1)S(1)}, u32[]{:S(2)}, u32[]{:S(2)}) %all-to-all-start.2) | async-done | bytes 65568 | tf_op jit(solution)/shard_map/all_to_all | solution.py:364
  61.3 0.0 copy-start.9
  61.3 0.0 copy-done.4
  61.3 0.7 copy-done.9
  62.0 4.9 %finish.1 = (bf16[12,264,128]{2,1,0:T(8,128)(2,1)}, bf16[12,264,128]{2,1,0:T(8,128)(2,1)}) custom-call(s32[16]{0:T(128)S(1)} %copy-done.7, bf16[32,8,128]{2,1,0:T(8,128)(2,1)S(1)} %all-to-all-done.2.c_ref, bf16[8,768]{1,0:T(8,128)(2,1)S(1)} %get-tuple-element.11.keep_ref, bf16[8,768]{1,0:T(8,128)(2,1)S(1)} %collective-permute-done.got_ref, ...), custom_call_target="tpu_custom_call" | custom-call | flops 600000000 | bytes 4110144 | tf_op jit(solution)/shard_map/finish/pallas_call | solution.py:313
  (5 shorter events, 0.0 us)
Async XLA Ops:
  0.6 1.1 %copy-start = (bf16[3,4,264,128]{3,2,1,0:T(8,128)(2,1)S(1)}, bf16[3,4,264,128]{3,2,1,0:T(8,128)(2,1)}, u32[]{:S(2)}) copy-start(bf16[3,4,264,128]{3,2,1,0:T(8,128)(2,1)} %param.13) | copy-start | bytes 2433028
  1.8 0.9 %copy-start.5 = (bf16[132,2,128]{2,1,0:T(2,128)(2,1)S(1)}, bf16[132,2,128]{2,1,0:T(2,128)(2,1)}, u32[]{:S(2)}) copy-start(bf16[132,2,128]{2,1,0:T(2,128)(2,1)} %param.20) | copy-start | bytes 202756
  2.7 12.2 %copy-start.1 = (bf16[3,4,264,128]{3,2,1,0:T(8,128)(2,1)S(1)}, bf16[3,4,264,128]{3,2,1,0:T(8,128)(2,1)}, u32[]{:S(2)}) copy-start(bf16[3,4,264,128]{3,2,1,0:T(8,128)(2,1)} %param.13) | copy-start | bytes 2433028
  4.1 10.6 %copy-start.13 = (f32[264]{0:T(512)S(1)}, f32[264]{0:T(512)}, u32[]{:S(2)}) copy-start(f32[264]{0:T(512)} %param.18) | copy-start | bytes 3172
  4.1 19.5 %all-to-all-start = ((bf16[32,8,128]{2,1,0:T(8,128)(2,1)}), bf16[32,8,128]{2,1,0:T(8,128)(2,1)S(1)}, u32[]{:S(2)}, u32[]{:S(2)}) async-start(bf16[32,8,128]{2,1,0:T(8,128)(2,1)} %x_partial.1), calls=%async_computation | async-start | bytes 131072 | tf_op jit(solution)/shard_map/all_to_all | solution.py:342
  14.8 0.7 copy-start.7
  14.8 0.7 copy-start.8
  15.5 1.0 %copy-start.2 = (bf16[268,2,264]{0,2,1:T(8,128)(2,1)S(1)}, bf16[268,2,264]{0,2,1:T(8,128)(2,1)}, u32[]{:S(2)}) copy-start(bf16[268,2,264]{0,2,1:T(8,128)(2,1)} %param.23) | copy-start | bytes 849028
  18.2 17.8 %copy-start.6 = (bf16[132,2,128]{2,1,0:T(2,128)(2,1)S(1)}, bf16[132,2,128]{2,1,0:T(2,128)(2,1)}, u32[]{:S(2)}) copy-start(bf16[132,2,128]{2,1,0:T(2,128)(2,1)} %param.20) | copy-start | bytes 202756
  18.2 17.8 %copy-start.10 = (f32[2,64,64]{2,1,0:T(8,128)S(1)}, f32[2,64,64]{2,1,0:T(8,128)}, u32[]{:S(2)}) copy-start(f32[2,64,64]{2,1,0:T(8,128)} %coupling_ref.2) | copy-start | bytes 98308
  23.6 23.5 %all-to-all-start.1 = ((bf16[16,56,128]{2,1,0:T(8,128)(2,1)}), bf16[16,56,128]{2,1,0:T(8,128)(2,1)S(1)}, u32[]{:S(2)}, u32[]{:S(2)}) async-start(bf16[16,56,128]{2,1,0:T(8,128)(2,1)} %y_partial.1), calls=%async_computation.1 | async-start | bytes 458752 | tf_op jit(solution)/shard_map/all_to_all | solution.py:358
  36.1 15.6 %copy-start.11 = (f32[2,32,32]{2,1,0:T(8,128)S(1)}, f32[2,32,32]{2,1,0:T(8,128)}, u32[]{:S(2)}) copy-start(f32[2,32,32]{2,1,0:T(8,128)} %coupling_ref.3) | copy-start | bytes 24580
  36.1 18.0 %copy-start.14 = (f32[264]{0:T(512)S(1)}, f32[264]{0:T(512)}, u32[]{:S(2)}) copy-start(f32[264]{0:T(512)} %param.19) | copy-start | bytes 3172
  36.1 18.0 %copy-start.12 = (f32[1,2,2,264]{3,2,1,0:T(2,128)S(1)}, f32[1,2,2,264]{3,2,1,0:T(2,128)}, u32[]{:S(2)}) copy-start(f32[1,2,2,264]{3,2,1,0:T(2,128)} %param.25) | copy-start | bytes 12676
  36.1 18.0 %copy-start.15 = (f32[2,2,128]{2,1,0:T(2,128)S(1)}, f32[2,2,128]{2,1,0:T(2,128)}, u32[]{:S(2)}) copy-start(f32[2,2,128]{2,1,0:T(2,128)} %param.22) | copy-start | bytes 6148
  36.1 25.2 %copy-start.4 = (bf16[3,4,264,128]{3,2,1,0:T(8,128)(2,1)S(1)}, bf16[3,4,264,128]{3,2,1,0:T(8,128)(2,1)}, u32[]{:S(2)}) copy-start(bf16[3,4,264,128]{3,2,1,0:T(8,128)(2,1)} %param.14) | copy-start | bytes 2433028
  36.5 17.6 %copy-start.3 = (bf16[268,2,264]{0,2,1:T(8,128)(2,1)S(1)}, bf16[268,2,264]{0,2,1:T(8,128)(2,1)}, u32[]{:S(2)}) copy-start(bf16[268,2,264]{0,2,1:T(8,128)(2,1)} %param.23) | copy-start | bytes 849028
  47.8 13.6 %all-to-all-start.2 = ((bf16[32,8,128]{2,1,0:T(8,128)(2,1)}), bf16[32,8,128]{2,1,0:T(8,128)(2,1)S(1)}, u32[]{:S(2)}, u32[]{:S(2)}) async-start(bf16[32,8,128]{2,1,0:T(8,128)(2,1)} %top.1), calls=%async_computation.2 | async-start | bytes 131072 | tf_op jit(solution)/shard_map/all_to_all | solution.py:364
  52.1 3.1 %collective-permute-start = (bf16[8,768]{1,0:T(8,128)(2,1)S(1)}, bf16[8,768]{1,0:T(8,128)(2,1)S(1)}, u32[]{:S(2)}, u32[]{:S(2)}) collective-permute-start(bf16[8,768]{1,0:T(8,128)(2,1)S(1)} %get-tuple-element.12), channel_id=1, source_target_pairs={{0,32},{32,0},{1,33},{33,1},{2,34},{34,2},{3,35},{35,3},{4,36},{36... | collective-permute-start | bytes 36872 | tf_op jit(solution)/shard_map/ppermute | solution.py:372
  61.3 0.7 copy-start.9

commit v2 on v1

--- a/solution.py
+++ b/solution.py
@@ -26,6 +26,8 @@
 CHUNKS = -(-LINES // CHUNK)
 HALF = NP // 2
 TILES = HALF + 1
+PIECE = 4 * CHUNK
+PIECES = -(-(LINES - PIECE) // PIECE)
 EDGE_X = (0, 1, XW - 2, XW - 1)
 HALO_X = (0, 1, XW + 2, XW + 3)
 
@@ -79,22 +81,39 @@
     return jnp.concatenate([pieces[0], pieces[1], pieces[2][0 : YR - 256]], axis=0)
 
 
-def x_partial_kernel(v_ref, x_ref, o_ref):
+def x_partial_kernel(
+    v_hbm, x_hbm, w_hbm, xs_hbm, ys_hbm, count_hbm,
+    o_ref, v_ref, x_ref, w_ref, xs_ref, ys_ref, count_ref, counts, sems,
+):
+    copies = [pltpu.make_async_copy(x_hbm, x_ref, sems.at[0])]
+    starts = list(range(0, LINES - PIECE, PIECE)) + [LINES]
+    starts[-2:] = [starts[-2], LINES]
+    for j in range(len(starts) - 1):
+        rows = pl.ds(starts[j], starts[j + 1] - starts[j])
+        copies.append(pltpu.make_async_copy(v_hbm.at[rows, :], v_ref.at[rows, :], sems.at[j + 1]))
+    later = ((w_hbm, w_ref), (xs_hbm, xs_ref), (ys_hbm, ys_ref), (count_hbm, counts))
+    later = [pltpu.make_async_copy(*pair, sems.at[len(starts) + j]) for j, pair in enumerate(later)]
+    for copy in copies + later:
+        copy.start()
     row, lane = iota((8, XW), 0), iota((8, XW), 1)
     pick = ones_where((row < 4) & (lane == (XW - 1) * (row % 2))).astype(BF16)
-    ends = nt(pick, x_ref[...])
     row_e = iota((8, 2 * (XW + 4)), 0)
-    weights = jnp.where(row == 4, ones_where(lane == EDGE_X[0]), F32(0.0))
+    edges = jnp.where(row == 4, ones_where(lane == EDGE_X[0]), F32(0.0))
     for j in range(1, 4):
-        weights = jnp.where(row == 4 + j, ones_where(lane == EDGE_X[j]), weights)
+        edges = jnp.where(row == 4 + j, ones_where(lane == EDGE_X[j]), edges)
     src, dst = iota((2 * (XW + 4), XW), 0), iota((2 * (XW + 4), XW), 1)
-    for k in range(2):
-        spread = ones_where(src == 2 * (dst + 2) + k).astype(BF16)
-        mine = jnp.where((row_e // 2) == k, ends, F32(0.0)).astype(BF16)
-        weights = weights + nn(mine, spread)
-    weights = weights.astype(BF16)
+    spread = ones_where(src // 2 == dst + 2).astype(BF16)
+    mine = iota((8, 2 * (XW + 4)), 1) % 2 == row_e // 2
+    copies[0].wait()
+    ends = jnp.where(mine, nt(pick, x_ref[...]), F32(0.0)).astype(BF16)
+    weights = (edges + nn(ends, spread)).astype(BF16)
+    arrived = 0
     for d in range(NCOL):
         first = CHUNK * d
+        last = min(first + 128, LINES)
+        while arrived < len(starts) - 1 and starts[arrived] < last:
+            arrived += 1
+            copies[arrived].wait()
         if first + 128 <= LINES:
             o_ref[d] = nt(weights, v_ref[first : first + 128, :]).astype(BF16)
         elif first < LINES:
@@ -103,10 +122,13 @@
             o_ref[d] = jnp.concatenate([part, rest], axis=1).astype(BF16)
         else:
             o_ref[d] = jnp.zeros((8, 128), BF16)
+    for copy in later:
+        copy.wait()
+    count_ref[...] = jnp.full((8, 128), counts[row_pos()], jnp.int32)
 
 
 def y_partial_kernel(count_ref, v_ref, w_ref, xs_ref, ys_ref, o_ref, pad_ref):
-    count = count_ref[row_pos()]
+    count = count_ref[0:1, 0:1]
     row, slot = iota((8, YR), 0), iota((8, YR), 1)
     place = jnp.where(row % 2 == 0, 0, count - 1)
     ends = nn(ones_where((row < 2) & (slot == place)).astype(BF16), w_ref[0])
@@ -115,7 +137,7 @@
     )
     pad_ref[...] = jnp.zeros_like(pad_ref)
     pad_ref[0:8, 0 : YR + 4] = ends
-    pad_ref[8:9, 0:YR] = ys_ref[...]
+    pad_ref[8:9, 0:YR] = ys_ref[...].reshape(1, YR)
     wide = pad_ref[0:8, :]
     own = pltpu.roll(wide, 384 - 2, 1)[:, 0:YR]
     edge = jnp.where(
@@ -167,13 +189,15 @@
     o_ref[...] = a_ref[...].reshape(NCOL, 8, 128).astype(BF16)
 
 
-def top_kernel(s_ref, r_ref, o_ref):
-    last = r_ref[...][:, 8 * HALF : 8 * TILES, :].astype(F32)
-    row = iota((NROW, 8, 128), 1)
-    parts = jnp.where((row >= 4) & (row < 7), last, F32(0.0))
-    top = jnp.max(jnp.sum(parts, axis=1), axis=0, keepdims=True)
+def top_of(ref, first, count, stride):
+    parts = [ref[pl.ds(first + j, count, stride=stride), :] for j in range(3)]
+    return jnp.max(parts[0] + parts[1] + parts[2], axis=0, keepdims=True)
+
+
+def top_kernel(s_ref, r_ref, after_ref, o_ref, t_ref):
+    t_ref[...] = r_ref[...][:, 8 * HALF : 8 * TILES, :].astype(F32).reshape(8 * NROW, 128)
+    tile = max_tile(top_of(t_ref, 4, NROW, 8))
     spare = iota((8, 128), 1) >= CHUNK
-    tile = max_tile(top)
     o_ref[...] = jnp.where(spare[None], tile[None], s_ref[...].astype(F32)).astype(BF16)
 
 
@@ -215,11 +239,11 @@
         out[...] = jnp.concatenate(pieces, axis=0).astype(BF16)
 
 
-def prepare_kernel(
-    count_ref, x_ref, xb_ref, w_ref, yb_ref, ys_ref, yc_ref,
-    xo_ref, xc_ref, wm_ref, hc_ref, yy_ref, pad_ref,
+def own_kernel(
+    count_ref, v_ref, x_ref, xb_ref, w_ref, yb_ref, xs_ref, xv_ref, ys_ref, yc_ref,
+    after_ref, own_ref, xc_ref, hc_ref, xx_ref, yy_ref, xo_ref, wm_ref,
 ):
-    count = count_ref[row_pos()]
+    count = count_ref[0:1, 0:1]
     x_all = x_ref[...]
     n_in = 2 * (XW + 4)
     dst, src = iota((XW, n_in), 0), iota((XW, n_in), 1)
@@ -251,33 +275,33 @@
         head = jnp.where(mine, y_high, F32(0.0)) + nt(pick_y, w_ref[k])
         tail = jnp.where(mine, yb_ref[...] - y_high, F32(0.0))
         hc_ref[k] = jnp.concatenate([head, tail], axis=0).astype(BF16)
-    pad_ref[...] = jnp.zeros_like(pad_ref)
-    pad_ref[0:1, 0:YR] = ys_ref[...]
-    pad_ref[1:2, 0:YR] = yc_ref[...]
-    scale = column_tiles(pad_ref, 0)
-    yy_ref[0] = scale
-    yy_ref[1] = viscosity * column_tiles(pad_ref, 1)
-    yy_ref[2] = viscosity * scale * scale
-
-
-def finish_kernel(
-    count_ref, c_ref, keep_ref, got_ref, v_ref, p_ref, xs_ref, xv_ref,
-    xo_ref, xc_ref, wm_ref, hc_ref, yy_ref, rhs_ref, inc_ref, x_add,
-):
-    count = count_ref[row_pos()]
-    core = lax.axis_index("row_1")
-    row, lane = iota((NCOL, 8, 128), 1), iota((NCOL, 8, 128), 2)
-    tops = jnp.where((lane >= CHUNK) & (row < 3), c_ref[...].astype(F32), F32(0.0))
-    top = jnp.max(jnp.sum(tops, axis=1), axis=0, keepdims=True)
-    step = cfl_target / (jnp.max(top, axis=1, keepdims=True) + 1e-06)
-    x_corr = xc_ref[...]
-    for d in range(CHUNKS):
-        coef = c_ref[d].astype(F32)
-        coef = jnp.concatenate([coef, coef], axis=0).astype(BF16)
-        x_add[CHUNK * d : CHUNK * d + 128, :] = tn(coef, x_corr)
-    live = iota((YR, XW), 0) < count
+    yy_ref[...] = jnp.zeros_like(yy_ref)
+    ys = ys_ref[...].reshape(1, YR)
+    yy_ref[0:1, 0:YR] = ys
+    yy_ref[1:2, 0:YR] = viscosity * yc_ref[...].reshape(1, YR)
+    yy_ref[2:3, 0:YR] = viscosity * ys * ys
+    scale, curv, y_second = (column_tiles(yy_ref, j) for j in range(3))
     xs, xv = xs_ref[...], viscosity * xv_ref[...]
     x_second = viscosity * xs * xs
+    xx_ref[...] = jnp.concatenate([xs, xv, x_second, jnp.zeros((5, XW), F32)], axis=0)
+    for pair in range(2):
+        for f in range(3):
+            plane = 4 * f + 2 * pair
+            both = jnp.concatenate([v_ref[plane], v_ref[plane + 1]], axis=1)
+            of_first, of_second = nn(wm_ref[0], both), nn(wm_ref[1], both)
+            for j in range(2):
+                p, z = plane + j, 2 * pair + j
+                at = slice(XW * j, XW * j + XW)
+                in_x = nn(v_ref[p], xo_ref[...])
+                u, v = v_ref[z].astype(F32), v_ref[4 + z].astype(F32)
+                rhs = (xv - u * xs) * in_x[:, 0:XW] + x_second * in_x[:, XW:]
+                rhs = rhs + (curv - v * scale) * of_first[:, at]
+                own_ref[p] = rhs + y_second * of_second[:, at]
+
+
+def y_add_kernel(keep_ref, got_ref, v_ref, own_ref, hc_ref, yy_ref, o_ref):
+    scale, curv, y_second = (column_tiles(yy_ref, j) for j in range(3))
+    core = lax.axis_index("row_1")
     for pair in range(2):
         for f in range(3):
             plane = 4 * f + 2 * pair
@@ -285,39 +309,67 @@
             lanes = slice(128 * g, 128 * g + 256)
             coef = jnp.where(core == half, keep_ref[:, lanes].astype(F32), got_ref[:, lanes].astype(F32))
             coef = jnp.concatenate([coef, coef], axis=0).astype(BF16)
-            both = jnp.concatenate([v_ref[plane], v_ref[plane + 1]], axis=1)
-            y_first = nn(wm_ref[0], both) + tn(hc_ref[0], coef)
-            y_second = nn(wm_ref[1], both) + tn(hc_ref[1], coef)
+            of_first, of_second = tn(hc_ref[0], coef), tn(hc_ref[1], coef)
             for j in range(2):
                 p, z = plane + j, 2 * pair + j
-                at = slice(128 * j, 128 * j + 128)
-                in_x = nn(v_ref[p], xo_ref[...]) + x_add[YR * p : YR * p + YR, :]
-                u, v = v_ref[z].astype(F32), v_ref[4 + z].astype(F32)
-                rhs = (xv - u * xs) * in_x[:, 0:XW] + x_second * in_x[:, XW:]
-                rhs = rhs + (yy_ref[1] - v * yy_ref[0]) * y_first[:, at] + yy_ref[2] * y_second[:, at]
-                rhs = jnp.where(live, rhs, F32(0.0))
-                inc = step * (gamma_coef * rhs + zeta_coef * p_ref[p].astype(F32))
-                inc = jnp.where(live, inc, F32(0.0))
-                rhs_ref[p] = rhs.astype(BF16)
-                inc_ref[p] = inc.astype(BF16)
+                at = slice(XW * j, XW * j + XW)
+                v = v_ref[4 + z].astype(F32)
+                add = (curv - v * scale) * of_first[:, at] + y_second * of_second[:, at]
+                o_ref[p] = own_ref[p] + add
+
+
+def finish_kernel(
+    count_ref, c_ref, v_ref, p_ref, base_ref, xc_ref, xx_ref, rhs_hbm, inc_hbm,
+    x_add, t_ref, rhs_ref, inc_ref, sems,
+):
+    count = count_ref[0:1, 0:1]
+    t_ref[...] = c_ref[...].astype(F32).reshape(8 * NCOL, 128)
+    top = top_of(t_ref, 0, NCOL, 8)
+    spare = iota((1, 128), 1) >= CHUNK
+    top = jnp.max(jnp.where(spare, top, F32(0.0)), axis=1, keepdims=True)
+    step = cfl_target / (top + 1e-06)
+    x_corr = xc_ref[...]
+    live = iota((YR, XW), 0) < count
+    xs, xv, x_second = xx_ref[0:1, :], xx_ref[1:2, :], xx_ref[2:3, :]
+    done, copies = 0, []
+    for p in range(NP):
+        while done < CHUNKS and CHUNK * done < YR * (p + 1):
+            coef = t_ref[8 * done : 8 * done + 8, :]
+            coef = jnp.concatenate([coef, coef], axis=0).astype(BF16)
+            x_add[CHUNK * done : CHUNK * done + 128, :] = tn(coef, x_corr)
+            done += 1
+        u = v_ref[p % 4].astype(F32)
+        add = x_add[YR * p : YR * p + YR, :]
+        rhs = base_ref[p] + (xv - u * xs) * add[:, 0:XW] + x_second * add[:, XW:]
+        rhs = jnp.where(live, rhs, F32(0.0))
+        inc = step * (gamma_coef * rhs + zeta_coef * p_ref[p].astype(F32))
+        rhs_ref[p] = rhs.astype(BF16)
+        inc_ref[p] = jnp.where(live, inc, F32(0.0)).astype(BF16)
+        for j, (source, target) in enumerate(((rhs_ref, rhs_hbm), (inc_ref, inc_hbm))):
+            copies.append(pltpu.make_async_copy(source.at[p], target.at[p], sems.at[j, p]))
+            copies[-1].start()
+    for copy in copies:
+        copy.wait()
 
 
 VMEM = pl.BlockSpec(memory_space=pltpu.VMEM)
-SMEM = pl.BlockSpec(memory_space=pltpu.SMEM)
-
-
-def call(body, name, operands, outs, scratch=(), flops=0, mib=16):
-    specs = [SMEM if operand.dtype == jnp.int32 else VMEM for operand in operands]
-    size = sum(o.size * o.dtype.itemsize for o in (*operands, *outs))
+HBM = pl.BlockSpec(memory_space=pltpu.HBM)
+
+
+def call(body, name, operands, outs, scratch=(), flops=0, mib=6, far=(), far_out=False, alias=None):
+    specs = [HBM if j in far else VMEM for j in range(len(operands))]
+    size = sum(o.size * o.dtype.itemsize for o in operands)
     single = len(outs) == 1
+    out_spec = HBM if far_out else VMEM
     return pl.pallas_call(
         body,
         out_shape=outs[0] if single else outs,
         in_specs=specs,
-        out_specs=VMEM if single else [VMEM] * len(outs),
-        scratch_shapes=[pltpu.VMEM(shape, F32) for shape in scratch],
+        out_specs=out_spec if single else [out_spec] * len(outs),
+        scratch_shapes=[pltpu.VMEM(item, F32) if isinstance(item, tuple) else item for item in scratch],
         compiler_params=pltpu.CompilerParams(vmem_limit_bytes=mib * 2**20),
         cost_estimate=pl.CostEstimate(flops=flops, bytes_accessed=size, transcendentals=0),
+        input_output_aliases=alias or {},
         name=name,
     )(*operands)
 
@@ -331,36 +383,52 @@
     x_local, x_coupling, x_basis, y_local, y_coupling, y_basis,
 ):
     lines = velocity.reshape(LINES, XW)
-    planes = velocity.reshape(NP, YR, XW)
     previous = rhs_prev.reshape(NP, YR, XW)
     x_rows = x_local.reshape(2 * (XW + 4), XW)
     y_mats = jnp.transpose(y_local, (1, 2, 0))
     x_scale, x_curv = x_scale.reshape(1, XW), x_curv.reshape(1, XW)
-    y_scale, y_curv = y_scale.reshape(1, YR), y_curv.reshape(1, YR)
-
-    mine = call(x_partial_kernel, "x_partial", (lines, x_rows), (shape((NCOL, 8, 128)),), flops=10**8)
+
+    fetched = (lines, x_rows, y_mats, x_scale, y_scale)
+    *fetched, row_counts = [
+        pltpu.with_memory_space_constraint(item, pltpu.HBM) for item in (*fetched, row_counts)
+    ]
+    mine, lines, x_rows, y_mats, x_scale, y_scale, count = call(
+        x_partial_kernel, "x_partial", (*fetched, row_counts),
+        (
+            shape((NCOL, 8, 128)), *(pltpu.VMEM(item.shape, item.dtype) for item in fetched),
+            pltpu.VMEM((8, 128), jnp.int32),
+        ),
+        (pltpu.SMEM((NROW,), jnp.int32), pltpu.SemaphoreType.DMA((PIECES + 5,))),
+        flops=10**8, far=range(6),
+    )
+    planes = lines.reshape(NP, YR, XW)
     theirs = lax.all_to_all(mine, COL, 0, 0, tiled=True)
     y_part = call(
-        y_partial_kernel, "y_partial", (row_counts, planes, y_mats, x_scale, y_scale),
+        y_partial_kernel, "y_partial", (count, planes, y_mats, x_scale, y_scale),
         (shape((NROW, 8 * TILES, 128)),), ((16, 384),), flops=10**8,
     )
     x_basis = jnp.pad(x_basis.reshape(4, XW), ((0, 4), (0, 0)))
     y_basis = jnp.pad(y_basis.reshape(4, YR), ((0, 4), (0, 0)))
-    prepared = call(
-        prepare_kernel, "prepare",
-        (row_counts, x_rows, x_basis, y_mats, y_basis, y_scale, y_curv),
-        (
-            shape((XW, 2 * XW)), shape((16, 2 * XW)), shape((2, YR, YR)),
-            shape((2, 16, YR)), shape((3, YR, XW), F32),
-        ),
-        ((8, 384),), flops=10**8,
-    )
     columns = lax.all_to_all(y_part, ROW, 0, 0, tiled=True)
     x_solved = call(
         x_solve_kernel, "x_solve", (theirs, x_rows, x_coupling), (shape((NCOL, 8, 128)),),
         ((NCOL * 8, 128), (2, 2 * NCOL, 128), (2, 2 * NCOL, 128)), flops=10**8,
     )
-    x_back = call(top_kernel, "top", (x_solved, columns), (shape((NCOL, 8, 128)),))
+    own, x_corr, y_corr, x_lines, y_lines = call(
+        own_kernel, "own",
+        (count, planes, x_rows, x_basis, y_mats, y_basis, x_scale, x_curv, y_scale, y_curv,
+            y_part),
+        (
+            shape((NP, YR, XW), F32), shape((16, 2 * XW)), shape((2, 16, YR)),
+            shape((8, XW), F32), shape((8, 384), F32),
+        ),
+        (pltpu.VMEM((XW, 2 * XW), BF16), pltpu.VMEM((2, YR, YR), BF16)),
+        flops=6 * 10**8, mib=8, far=(10,),
+    )
+    x_back = call(
+        top_kernel, "top", (x_solved, columns, x_lines), (shape((NCOL, 8, 128)),),
+        ((8 * NROW, 128),), far=(2,),
+    )
     x_back = lax.all_to_all(x_back, COL, 0, 0, tiled=True)
     wide = 128 * HALF
     keep, send = call(
@@ -370,11 +438,19 @@
         ), flops=10**8,
     )
     got = lax.ppermute(send, "row_1", [(0, 1), (1, 0)])
+    base = call(
+        y_add_kernel, "y_add", (keep, got, planes, own, y_corr, y_lines),
+        (shape(own.shape, F32),), flops=10**8, alias={3: 0},
+    )
     rhs, inc = call(
         finish_kernel, "finish",
-        (row_counts, x_back, keep, got, planes, previous, x_scale, x_curv, *prepared),
+        (count, x_back, planes, previous, base, x_corr, x_lines),
         (shape((NP, YR, XW)), shape((NP, YR, XW))),
-        ((CHUNK * (CHUNKS - 1) + 128, 2 * XW),), flops=6 * 10**8, mib=32,
+        (
+            (CHUNK * (CHUNKS - 1) + 128, 2 * XW), (8 * NCOL, 128),
+            pltpu.VMEM((NP, YR, XW), BF16), pltpu.VMEM((NP, YR, XW), BF16),
+            pltpu.SemaphoreType.DMA((2, NP)),
+        ), flops=10**8, mib=10, far_out=True,
     )
     return rhs.reshape(velocity.shape), inc.reshape(velocity.shape)
 

time: 67.4 us -> 63.4 us (0.941)
  local copies, waits for them, and re-layouts: 4.4 us -> 0.06 us
    unnamed x32 -> x14, local copies, waits for them, and re-layouts: 4.37 us -> 0.03 us
    all_to_all x1, waiting for transfers between devices: 5.38 us -> 7.6 us  [shards(): theirs = lax.all_to_all(mine, COL, 0, 0, tiled=True)]
    all_to_all x1, waiting for transfers between devices: 10.6 us -> 8.57 us  [shards(): columns = lax.all_to_all(y_part, ROW, 0, 0, tiled=True)]
    ppermute x1, waiting for transfers between devices: 0.01 us -> 1.14 us  [shards(): got = lax.ppermute(send, 'row_1', [(0, 1), (1, 0)])]
    all_to_all x1, waiting for transfers between devices: 6.14 us -> 5.09 us  [shards(): x_back = lax.all_to_all(x_back, COL, 0, 0, tiled=True)]
    pallas_call x7 -> x8, Pallas kernels: 10.6 us -> 11.1 us  [call(): pl.pallas_call(body, out_shape=outs[0] if single else outs, in_specs=spec...]
  transfers between devices with their start and end apart: 4 -> 4, of which waited for: 3 -> 4; matrix products, arithmetic and copies ran while one was open for 0% -> 0% of each run, Pallas kernels for 5% -> 8%
where the time goes in v2:
time: 63.4 us; the launch traced here: 63.1 us
  starting transfers between devices  28.7 us (45%)
  waiting for transfers between devices  22.4 us (35%)
  Pallas kernels  11.1 us (18%)
  between operations  0.8 us (1%)
    all_to_all x1, starting transfers between devices, shards(): columns = lax.all_to_all(y_part, ROW, 0, 0, tiled=True)  12.4 us
    pallas_call x8, Pallas kernels, call(): pl.pallas_call(body, out_shape=outs[0] if single else outs, in_specs=spec...  11.1 us
    all_to_all x1, starting transfers between devices, shards(): theirs = lax.all_to_all(mine, COL, 0, 0, tiled=True)  10.5 us
    all_to_all x1, waiting for transfers between devices, shards(): columns = lax.all_to_all(y_part, ROW, 0, 0, tiled=True)  8.57 us
    all_to_all x1, waiting for transfers between devices, shards(): theirs = lax.all_to_all(mine, COL, 0, 0, tiled=True)  7.6 us
    all_to_all x1, waiting for transfers between devices, shards(): x_back = lax.all_to_all(x_back, COL, 0, 0, tiled=True)  5.09 us
    all_to_all x1, starting transfers between devices, shards(): x_back = lax.all_to_all(x_back, COL, 0, 0, tiled=True)  3.86 us
    ppermute x1, starting transfers between devices, shards(): got = lax.ppermute(send, 'row_1', [(0, 1), (1, 0)])  1.92 us
  transfers between devices with their start and end apart: 4, of which 4 were waited for; matrix products, arithmetic and copies ran while one was open for 0% of the time, Pallas kernels for 8%

profile of v2, /device:TPU:1, one launch (start us, length us, event | category | flops | bytes accessed | tf_op | source)
XLA Modules:
  0.0 63.1 jit_solution(4956513104976797105)
XLA Ops:
  0.6 0.0 copy-start.5
  0.6 0.0 copy-start.6
  0.7 0.0 copy-start.3
  0.7 0.0 copy-start.4
  0.7 3.2 %x_partial.1 = (bf16[32,8,128]{2,1,0:T(8,128)(2,1)}, bf16[3168,128]{1,0:T(8,128)(2,1)S(1)}, bf16[264,128]{1,0:T(8,128)(2,1)S(1)}, bf16[2,264,268]{2,1,0:T(8,128)...) custom-call(bf16[3168,128]{1,0:T(8,128)(2,1)} %bitcast.16, bf16[264,128]{1,0:T(8,128)(2,1)} %bitcast.18, ...), custom_call_target="tpu_custom_call" | custom-call | flops 100000000 | bytes 1163232 | tf_op jit(solution)/shard_map/x_partial/pallas_call | solution.py:364
  3.9 10.5 %all-to-all-start = ((bf16[32,8,128]{2,1,0:T(8,128)(2,1)}), bf16[32,8,128]{2,1,0:T(8,128)(2,1)S(1)}, u32[]{:S(2)}, u32[]{:S(2)}) async-start(bf16[32,8,128]{2,1,0:T(8,128)(2,1)} %get-tuple-element.19), calls=%async_computation | async-start | bytes 131072 | tf_op jit(solution)/shard_map/all_to_all | solution.py:405
  14.4 1.2 %y_partial.1.after_ref = bf16[16,56,128]{2,1,0:T(8,128)(2,1)} custom-call(s32[8,128]{1,0:T(8,128)S(1)} %get-tuple-element.18.count_ref, bf16[12,264,128]{2,1,0:T(8,128)(2,1)S(1)} %bitcast.10, bf16[2,264,268]{2,1,0:T(8,128)(2,1)S(1)} %get-tuple-element.22.w_ref, f32[1,128]{1,0:T(1,128)S(1)} %get-tuple-element.23.xs_ref, f32[264]{0:T(512)S(1)} %get-tuple-element.24.ys_ref), custom_call_target="tpu_custom_call" | custom-call | flops 100000000 | bytes 1099680 | tf_op jit(solution)/shard_map/y_partial/pallas_call | solution.py:364
  15.7 0.0 copy-start.1
  15.7 7.6 %all-to-all-done.c_ref = bf16[32,8,128]{2,1,0:T(8,128)(2,1)S(1)} async-done(((bf16[32,8,128]{2,1,0:T(8,128)(2,1)}), bf16[32,8,128]{2,1,0:T(8,128)(2,1)S(1)}, u32[]{:S(2)}, u32[]{:S(2)}) %all-to-all-start) | async-done | bytes 65568 | tf_op jit(solution)/shard_map/all_to_all | solution.py:405
  23.3 12.4 %all-to-all-start.1 = ((bf16[16,56,128]{2,1,0:T(8,128)(2,1)}), bf16[16,56,128]{2,1,0:T(8,128)(2,1)S(1)}, u32[]{:S(2)}, u32[]{:S(2)}) async-start(bf16[16,56,128]{2,1,0:T(8,128)(2,1)} %y_partial.1.after_ref), calls=%async_computation.1 | async-start | bytes 458752 | tf_op jit(solution)/shard_map/all_to_all | solution.py:412
  35.7 0.0 copy-done.5
  35.7 0.0 copy-start.2
  35.7 0.0 copy-done.6
  35.8 0.0 copy-done.3
  35.8 0.0 copy-done.4
  35.8 2.0 %own.1 = (f32[12,264,128]{2,1,0:T(8,128)S(1)}, bf16[16,256]{1,0:T(8,128)(2,1)S(1)}, bf16[2,16,264]{2,1,0:T(8,128)(2,1)S(1)}, f32[8,128]{1,0:T(8,128)S(1)}, f32[8,384]{1,0:T(8,128)S(1)}) custom-call(s32[8,128]{1,0:T(8,128)S(1)} %get-tuple-element.18.count_ref, bf16[12,264,128]{2,1,0:T(8,128)(2,1)S(1)} %bitcast.11, ...), custom_call_target="tpu_custom_call" | custom-call | flops 600000000 | bytes 1410752 | tf_op jit(solution)/shard_map/own/pallas_call | solution.py:364
  37.8 0.0 copy-done.1
  37.8 0.3 x_solve.1.s_ref
  38.2 8.6 %all-to-all-done.1.r_ref = bf16[16,56,128]{2,1,0:T(8,128)(2,1)S(1)} async-done(((bf16[16,56,128]{2,1,0:T(8,128)(2,1)}), bf16[16,56,128]{2,1,0:T(8,128)(2,1)S(1)}, u32[]{:S(2)}, u32[]{:S(2)}) %all-to-all-start.1) | async-done | bytes 229408 | tf_op jit(solution)/shard_map/all_to_all | solution.py:412
  46.7 0.7 %top.1 = bf16[32,8,128]{2,1,0:T(8,128)(2,1)} custom-call(bf16[32,8,128]{2,1,0:T(8,128)(2,1)S(1)} %x_solve.1.s_ref, bf16[16,56,128]{2,1,0:T(8,128)(2,1)S(1)} %all-to-all-done.1.r_ref, f32[8,128]{1,0:T(8,128)S(1)} %get-tuple-element.25.after_ref.xx_ref), custom_call_target="tpu_custom_call" | custom-call | bytes 299008 | tf_op jit(solution)/shard_map/top/pallas_call | solution.py:364
  47.4 3.9 %all-to-all-start.2 = ((bf16[32,8,128]{2,1,0:T(8,128)(2,1)}), bf16[32,8,128]{2,1,0:T(8,128)(2,1)S(1)}, u32[]{:S(2)}, u32[]{:S(2)}) async-start(bf16[32,8,128]{2,1,0:T(8,128)(2,1)} %top.1), calls=%async_computation.2 | async-start | bytes 131072 | tf_op jit(solution)/shard_map/all_to_all | solution.py:432
  51.3 0.0 copy-done.2
  51.3 0.5 y_solve.1
  51.8 1.9 %collective-permute-start = (bf16[8,768]{1,0:T(8,128)(2,1)S(1)}, bf16[8,768]{1,0:T(8,128)(2,1)S(1)}, u32[]{:S(2)}, u32[]{:S(2)}) collective-permute-start(bf16[8,768]{1,0:T(8,128)(2,1)S(1)} %get-tuple-element.27), channel_id=1, source_target_pairs={{0,32},{32,0},{1,33},{33,1},{2,34},{34,2},{3,35},{35,3},{4,36},{36... | collective-permute-start | bytes 36872 | tf_op jit(solution)/shard_map/ppermute | solution.py:440
  53.7 1.1 %collective-permute-done.got_ref = bf16[8,768]{1,0:T(8,128)(2,1)S(1)} collective-permute-done((bf16[8,768]{1,0:T(8,128)(2,1)S(1)}, bf16[8,768]{1,0:T(8,128)(2,1)S(1)}, u32[]{:S(2)}, u32[]{:S(2)}) %collective-permute-start) | collective-permute-done | bytes 12320 | tf_op jit(solution)/shard_map/ppermute | solution.py:440
  54.8 0.0 copy-start
  54.8 1.1 %y_add.1.base_ref = f32[12,264,128]{2,1,0:T(8,128)S(1)} custom-call(bf16[8,768]{1,0:T(8,128)(2,1)S(1)} %get-tuple-element.26.keep_ref, bf16[8,768]{1,0:T(8,128)(2,1)S(1)} %collective-permute-done.got_ref, bf16[12,264,128]{2,1,0:T(8,128)(2,1)S(1)} %bitcast.12, f32[12,264,128]{2,1,0:T(8,128)S(1)} %get-tuple-element.28.own_ref, ...), custom_call_target="tpu_custom_call", output_to_operand_aliasing={{}: (3, {})} | custom-call | flops 100000000 | bytes 2486784 | tf_op jit(solution)/shard_map/y_add/pallas_call | solution.py:364
  55.9 5.1 %all-to-all-done.2.c_ref = bf16[32,8,128]{2,1,0:T(8,128)(2,1)S(1)} async-done(((bf16[32,8,128]{2,1,0:T(8,128)(2,1)}), bf16[32,8,128]{2,1,0:T(8,128)(2,1)S(1)}, u32[]{:S(2)}, u32[]{:S(2)}) %all-to-all-start.2) | async-done | bytes 65568 | tf_op jit(solution)/shard_map/all_to_all | solution.py:432
  61.0 0.0 copy-done
  61.0 2.1 %finish.1 = (bf16[12,264,128]{2,1,0:T(8,128)(2,1)}, bf16[12,264,128]{2,1,0:T(8,128)(2,1)}) custom-call(s32[8,128]{1,0:T(8,128)S(1)} %get-tuple-element.18.count_ref, bf16[32,8,128]{2,1,0:T(8,128)(2,1)S(1)} %all-to-all-done.2.c_ref, bf16[12,264,128]{2,1,0:T(8,128)(2,1)S(1)} %bitcast.13, bf16[12,264,128]{2,1,0:T(8,128)(2,1)S(1)} %bitcast.14, ...), custom_call_target="tpu_custom_call" | custom-call | flops 100000000 | bytes 3325952 | tf_op jit(solution)/shard_map/finish/pallas_call | solution.py:364
  (3 shorter events, 0.0 us)
Async XLA Ops:
  0.6 35.1 %copy-start.5 = (f32[1,2,2,264]{3,2,1,0:T(2,128)S(1)}, f32[1,2,2,264]{3,2,1,0:T(2,128)}, u32[]{:S(2)}) copy-start(f32[1,2,2,264]{3,2,1,0:T(2,128)} %param.25) | copy-start | bytes 12676
  0.6 35.1 %copy-start.6 = (f32[2,2,128]{2,1,0:T(2,128)S(1)}, f32[2,2,128]{2,1,0:T(2,128)}, u32[]{:S(2)}) copy-start(f32[2,2,128]{2,1,0:T(2,128)} %param.22) | copy-start | bytes 6148
  0.7 35.1 %copy-start.3 = (f32[264]{0:T(512)S(1)}, f32[264]{0:T(512)}, u32[]{:S(2)}) copy-start(f32[264]{0:T(512)} %yc_ref.1) | copy-start | bytes 3172
  0.7 35.1 %copy-start.4 = (f32[128]{0:T(128)S(1)}, f32[128]{0:T(128)}, u32[]{:S(2)}) copy-start(f32[128]{0:T(128)} %param.17) | copy-start | bytes 1540
  3.9 19.3 %all-to-all-start = ((bf16[32,8,128]{2,1,0:T(8,128)(2,1)}), bf16[32,8,128]{2,1,0:T(8,128)(2,1)S(1)}, u32[]{:S(2)}, u32[]{:S(2)}) async-start(bf16[32,8,128]{2,1,0:T(8,128)(2,1)} %get-tuple-element.19), calls=%async_computation | async-start | bytes 131072 | tf_op jit(solution)/shard_map/all_to_all | solution.py:405
  15.7 22.2 %copy-start.1 = (f32[2,64,64]{2,1,0:T(8,128)S(1)}, f32[2,64,64]{2,1,0:T(8,128)}, u32[]{:S(2)}) copy-start(f32[2,64,64]{2,1,0:T(8,128)} %coupling_ref.2) | copy-start | bytes 98308
  23.3 23.5 %all-to-all-start.1 = ((bf16[16,56,128]{2,1,0:T(8,128)(2,1)}), bf16[16,56,128]{2,1,0:T(8,128)(2,1)S(1)}, u32[]{:S(2)}, u32[]{:S(2)}) async-start(bf16[16,56,128]{2,1,0:T(8,128)(2,1)} %y_partial.1.after_ref), calls=%async_computation.1 | async-start | bytes 458752 | tf_op jit(solution)/shard_map/all_to_all | solution.py:412
  35.7 15.6 %copy-start.2 = (f32[2,32,32]{2,1,0:T(8,128)S(1)}, f32[2,32,32]{2,1,0:T(8,128)}, u32[]{:S(2)}) copy-start(f32[2,32,32]{2,1,0:T(8,128)} %coupling_ref.3) | copy-start | bytes 24580
  47.4 13.6 %all-to-all-start.2 = ((bf16[32,8,128]{2,1,0:T(8,128)(2,1)}), bf16[32,8,128]{2,1,0:T(8,128)(2,1)S(1)}, u32[]{:S(2)}, u32[]{:S(2)}) async-start(bf16[32,8,128]{2,1,0:T(8,128)(2,1)} %top.1), calls=%async_computation.2 | async-start | bytes 131072 | tf_op jit(solution)/shard_map/all_to_all | solution.py:432
  51.8 3.1 %collective-permute-start = (bf16[8,768]{1,0:T(8,128)(2,1)S(1)}, bf16[8,768]{1,0:T(8,128)(2,1)S(1)}, u32[]{:S(2)}, u32[]{:S(2)}) collective-permute-start(bf16[8,768]{1,0:T(8,128)(2,1)S(1)} %get-tuple-element.27), channel_id=1, source_target_pairs={{0,32},{32,0},{1,33},{33,1},{2,34},{34,2},{3,35},{35,3},{4,36},{36... | collective-permute-start | bytes 36872 | tf_op jit(solution)/shard_map/ppermute | solution.py:440
  54.8 6.2 %copy-start = (bf16[3,4,264,128]{3,2,1,0:T(8,128)(2,1)S(1)}, bf16[3,4,264,128]{3,2,1,0:T(8,128)(2,1)}, u32[]{:S(2)}) copy-start(bf16[3,4,264,128]{3,2,1,0:T(8,128)(2,1)} %param.14) | copy-start | bytes 2433028

commit v3 on v2

--- a/solution.py
+++ b/solution.py
@@ -1,3 +1,5 @@
+import functools
+
 import jax
 import jax.numpy as jnp
 from jax import lax
@@ -26,8 +28,7 @@
 CHUNKS = -(-LINES // CHUNK)
 HALF = NP // 2
 TILES = HALF + 1
-PIECE = 4 * CHUNK
-PIECES = -(-(LINES - PIECE) // PIECE)
+GROUP = 4
 EDGE_X = (0, 1, XW - 2, XW - 1)
 HALO_X = (0, 1, XW + 2, XW + 3)
 
@@ -85,14 +86,11 @@
     v_hbm, x_hbm, w_hbm, xs_hbm, ys_hbm, count_hbm,
     o_ref, v_ref, x_ref, w_ref, xs_ref, ys_ref, count_ref, counts, sems,
 ):
-    copies = [pltpu.make_async_copy(x_hbm, x_ref, sems.at[0])]
-    starts = list(range(0, LINES - PIECE, PIECE)) + [LINES]
-    starts[-2:] = [starts[-2], LINES]
-    for j in range(len(starts) - 1):
-        rows = pl.ds(starts[j], starts[j + 1] - starts[j])
-        copies.append(pltpu.make_async_copy(v_hbm.at[rows, :], v_ref.at[rows, :], sems.at[j + 1]))
+    copies = [
+        pltpu.make_async_copy(x_hbm, x_ref, sems.at[0]), pltpu.make_async_copy(v_hbm, v_ref, sems.at[1])
+    ]
     later = ((w_hbm, w_ref), (xs_hbm, xs_ref), (ys_hbm, ys_ref), (count_hbm, counts))
-    later = [pltpu.make_async_copy(*pair, sems.at[len(starts) + j]) for j, pair in enumerate(later)]
+    later = [pltpu.make_async_copy(*pair, sems.at[2 + j]) for j, pair in enumerate(later)]
     for copy in copies + later:
         copy.start()
     row, lane = iota((8, XW), 0), iota((8, XW), 1)
@@ -107,21 +105,19 @@
     copies[0].wait()
     ends = jnp.where(mine, nt(pick, x_ref[...]), F32(0.0)).astype(BF16)
     weights = (edges + nn(ends, spread)).astype(BF16)
-    arrived = 0
-    for d in range(NCOL):
+    o_ref[CHUNKS:] = jnp.zeros((NCOL - CHUNKS, 8, 128), BF16)
+    copies[1].wait()
+    for d in range(0, NCOL, 2):
         first = CHUNK * d
-        last = min(first + 128, LINES)
-        while arrived < len(starts) - 1 and starts[arrived] < last:
-            arrived += 1
-            copies[arrived].wait()
-        if first + 128 <= LINES:
-            o_ref[d] = nt(weights, v_ref[first : first + 128, :]).astype(BF16)
-        elif first < LINES:
-            part = nt(weights, v_ref[first:LINES, :])
-            rest = jnp.zeros((8, 128 - (LINES - first)), F32)
+        last = min(first + 256, LINES)
+        if last - first == 256:
+            pair = nt(weights, v_ref[first:last, :])
+            o_ref[d] = pair[:, 0:128].astype(BF16)
+            o_ref[d + 1] = pltpu.roll(pair, 256 - CHUNK, 1)[:, 0:128].astype(BF16)
+        elif last > first:
+            part = nt(weights, v_ref[first:last, :])
+            rest = jnp.zeros((8, 128 - (last - first)), F32)
             o_ref[d] = jnp.concatenate([part, rest], axis=1).astype(BF16)
-        else:
-            o_ref[d] = jnp.zeros((8, 128), BF16)
     for copy in later:
         copy.wait()
     count_ref[...] = jnp.full((8, 128), counts[row_pos()], jnp.int32)
@@ -299,23 +295,20 @@
                 own_ref[p] = rhs + y_second * of_second[:, at]
 
 
-def y_add_kernel(keep_ref, got_ref, v_ref, own_ref, hc_ref, yy_ref, o_ref):
+def y_add_kernel(other, coef_ref, v_ref, own_ref, hc_ref, yy_ref, o_ref):
+    core = lax.axis_index("row_1")
+    half = 1 - core if other else core
     scale, curv, y_second = (column_tiles(yy_ref, j) for j in range(3))
-    core = lax.axis_index("row_1")
-    for pair in range(2):
-        for f in range(3):
-            plane = 4 * f + 2 * pair
-            half, g = divmod(plane, HALF)
-            lanes = slice(128 * g, 128 * g + 256)
-            coef = jnp.where(core == half, keep_ref[:, lanes].astype(F32), got_ref[:, lanes].astype(F32))
-            coef = jnp.concatenate([coef, coef], axis=0).astype(BF16)
-            of_first, of_second = tn(hc_ref[0], coef), tn(hc_ref[1], coef)
-            for j in range(2):
-                p, z = plane + j, 2 * pair + j
-                at = slice(XW * j, XW * j + XW)
-                v = v_ref[4 + z].astype(F32)
-                add = (curv - v * scale) * of_first[:, at] + y_second * of_second[:, at]
-                o_ref[p] = own_ref[p] + add
+    for g in range(0, HALF, 2):
+        coef = coef_ref[:, 128 * g : 128 * g + 256].astype(F32)
+        coef = jnp.concatenate([coef, coef], axis=0).astype(BF16)
+        of_first, of_second = tn(hc_ref[0], coef), tn(hc_ref[1], coef)
+        for j in range(2):
+            p = HALF * half + g + j
+            at = slice(128 * j, 128 * j + 128)
+            v = v_ref[4 + lax.rem(p, 4)].astype(F32)
+            add = (curv - v * scale) * of_first[:, at] + y_second * of_second[:, at]
+            o_ref[p] = own_ref[p] + add
 
 
 def finish_kernel(
@@ -328,6 +321,7 @@
     spare = iota((1, 128), 1) >= CHUNK
     top = jnp.max(jnp.where(spare, top, F32(0.0)), axis=1, keepdims=True)
     step = cfl_target / (top + 1e-06)
+    gamma_step, zeta_step = gamma_coef * step, zeta_coef * step
     x_corr = xc_ref[...]
     live = iota((YR, XW), 0) < count
     xs, xv, x_second = xx_ref[0:1, :], xx_ref[1:2, :], xx_ref[2:3, :]
@@ -340,14 +334,17 @@
             done += 1
         u = v_ref[p % 4].astype(F32)
         add = x_add[YR * p : YR * p + YR, :]
-        rhs = base_ref[p] + (xv - u * xs) * add[:, 0:XW] + x_second * add[:, XW:]
-        rhs = jnp.where(live, rhs, F32(0.0))
-        inc = step * (gamma_coef * rhs + zeta_coef * p_ref[p].astype(F32))
+        rhs = (xv - u * xs) * add[:, 0:XW] + x_second * add[:, XW:]
+        rhs = jnp.where(live, base_ref[p] + rhs, F32(0.0))
+        before = jnp.where(live, zeta_step, F32(0.0)) * p_ref[p].astype(F32)
         rhs_ref[p] = rhs.astype(BF16)
-        inc_ref[p] = jnp.where(live, inc, F32(0.0)).astype(BF16)
-        for j, (source, target) in enumerate(((rhs_ref, rhs_hbm), (inc_ref, inc_hbm))):
-            copies.append(pltpu.make_async_copy(source.at[p], target.at[p], sems.at[j, p]))
-            copies[-1].start()
+        inc_ref[p] = (gamma_step * rhs + before).astype(BF16)
+        if (p + 1) % GROUP == 0:
+            group = pl.ds(p + 1 - GROUP, GROUP)
+            for j, (source, target) in enumerate(((rhs_ref, rhs_hbm), (inc_ref, inc_hbm))):
+                sem = sems.at[j, p // GROUP]
+                copies.append(pltpu.make_async_copy(source.at[group], target.at[group], sem))
+                copies[-1].start()
     for copy in copies:
         copy.wait()
 
@@ -356,16 +353,16 @@
 HBM = pl.BlockSpec(memory_space=pltpu.HBM)
 
 
-def call(body, name, operands, outs, scratch=(), flops=0, mib=6, far=(), far_out=False, alias=None):
+def call(body, name, operands, outs, scratch=(), flops=0, mib=6, far=(), far_outs=(), alias=None):
     specs = [HBM if j in far else VMEM for j in range(len(operands))]
     size = sum(o.size * o.dtype.itemsize for o in operands)
     single = len(outs) == 1
-    out_spec = HBM if far_out else VMEM
+    out_specs = [HBM if j in far_outs else VMEM for j in range(len(outs))]
     return pl.pallas_call(
         body,
         out_shape=outs[0] if single else outs,
         in_specs=specs,
-        out_specs=out_spec if single else [out_spec] * len(outs),
+        out_specs=out_specs[0] if single else out_specs,
         scratch_shapes=[pltpu.VMEM(item, F32) if isinstance(item, tuple) else item for item in scratch],
         compiler_params=pltpu.CompilerParams(vmem_limit_bytes=mib * 2**20),
         cost_estimate=pl.CostEstimate(flops=flops, bytes_accessed=size, transcendentals=0),
@@ -398,7 +395,7 @@
             shape((NCOL, 8, 128)), *(pltpu.VMEM(item.shape, item.dtype) for item in fetched),
             pltpu.VMEM((8, 128), jnp.int32),
         ),
-        (pltpu.SMEM((NROW,), jnp.int32), pltpu.SemaphoreType.DMA((PIECES + 5,))),
+        (pltpu.SMEM((NROW,), jnp.int32), pltpu.SemaphoreType.DMA((6,))),
         flops=10**8, far=range(6),
     )
     planes = lines.reshape(NP, YR, XW)
@@ -438,10 +435,13 @@
         ), flops=10**8,
     )
     got = lax.ppermute(send, "row_1", [(0, 1), (1, 0)])
-    base = call(
-        y_add_kernel, "y_add", (keep, got, planes, own, y_corr, y_lines),
-        (shape(own.shape, F32),), flops=10**8, alias={3: 0},
-    )
+    base = own
+    for other, coefs in enumerate((keep, got)):
+        base = call(
+            functools.partial(y_add_kernel, other), "y_add",
+            (coefs, planes, base, y_corr, y_lines),
+            (shape(own.shape, F32),), flops=10**8, alias={2: 0},
+        )
     rhs, inc = call(
         finish_kernel, "finish",
         (count, x_back, planes, previous, base, x_corr, x_lines),
@@ -449,8 +449,8 @@
         (
             (CHUNK * (CHUNKS - 1) + 128, 2 * XW), (8 * NCOL, 128),
             pltpu.VMEM((NP, YR, XW), BF16), pltpu.VMEM((NP, YR, XW), BF16),
-            pltpu.SemaphoreType.DMA((2, NP)),
-        ), flops=10**8, mib=10, far_out=True,
+            pltpu.SemaphoreType.DMA((2, NP // GROUP)),
+        ), flops=10**8, mib=10, far_outs=(0, 1),
     )
     return rhs.reshape(velocity.shape), inc.reshape(velocity.shape)
 

time: 63.4 us -> 62.3 us (0.983)
  Pallas kernels: 11.1 us -> 10.1 us
    pallas_call x8 -> x9, Pallas kernels: 11.1 us -> 10.1 us  [call(): pl.pallas_call(body, out_shape=outs[0] if single else outs, in_specs=spec...]
where the time goes in v3:
time: 62.3 us; the launch traced here: 62 us
  starting transfers between devices  28.7 us (46%)
  waiting for transfers between devices  22.3 us (36%)
  Pallas kernels  10.1 us (16%)
  between operations  0.81 us (1%)
    all_to_all x1, starting transfers between devices, shards(): columns = lax.all_to_all(y_part, ROW, 0, 0, tiled=True)  12.4 us
    all_to_all x1, starting transfers between devices, shards(): theirs = lax.all_to_all(mine, COL, 0, 0, tiled=True)  10.5 us
    pallas_call x9, Pallas kernels, call(): pl.pallas_call(body, out_shape=outs[0] if single else outs, in_specs=spec...  10.1 us
    all_to_all x1, waiting for transfers between devices, shards(): columns = lax.all_to_all(y_part, ROW, 0, 0, tiled=True)  8.58 us
    all_to_all x1, waiting for transfers between devices, shards(): theirs = lax.all_to_all(mine, COL, 0, 0, tiled=True)  7.6 us
    all_to_all x1, waiting for transfers between devices, shards(): x_back = lax.all_to_all(x_back, COL, 0, 0, tiled=True)  5.57 us
    all_to_all x1, starting transfers between devices, shards(): x_back = lax.all_to_all(x_back, COL, 0, 0, tiled=True)  3.86 us
    ppermute x1, starting transfers between devices, shards(): got = lax.ppermute(send, 'row_1', [(0, 1), (1, 0)])  1.92 us
  transfers between devices with their start and end apart: 4, of which 4 were waited for; matrix products, arithmetic and copies ran while one was open for 0% of the time, Pallas kernels for 8%

profile of v3, /device:TPU:1, one launch (start us, length us, event | category | flops | bytes accessed | tf_op | source)
XLA Modules:
  0.0 62.0 jit_solution(1376998949598780274)
XLA Ops:
  0.6 0.0 copy-start.5
  0.6 0.0 copy-start.6
  0.7 0.0 copy-start.3
  0.7 0.0 copy-start.4
  0.7 2.3 %x_partial.1 = (bf16[32,8,128]{2,1,0:T(8,128)(2,1)}, bf16[3168,128]{1,0:T(8,128)(2,1)S(1)}, bf16[264,128]{1,0:T(8,128)(2,1)S(1)}, bf16[2,264,268]{2,1,0:T(8,128)...) custom-call(bf16[3168,128]{1,0:T(8,128)(2,1)} %bitcast.17, bf16[264,128]{1,0:T(8,128)(2,1)} %bitcast.19, ...), custom_call_target="tpu_custom_call" | custom-call | flops 100000000 | bytes 1163232 | tf_op jit(solution)/shard_map/x_partial/pallas_call | solution.py:361
  3.0 10.5 %all-to-all-start = ((bf16[32,8,128]{2,1,0:T(8,128)(2,1)}), bf16[32,8,128]{2,1,0:T(8,128)(2,1)S(1)}, u32[]{:S(2)}, u32[]{:S(2)}) async-start(bf16[32,8,128]{2,1,0:T(8,128)(2,1)} %get-tuple-element.19), calls=%async_computation | async-start | bytes 131072 | tf_op jit(solution)/shard_map/all_to_all | solution.py:402
  13.5 1.2 %y_partial.1.after_ref = bf16[16,56,128]{2,1,0:T(8,128)(2,1)} custom-call(s32[8,128]{1,0:T(8,128)S(1)} %get-tuple-element.18.count_ref, bf16[12,264,128]{2,1,0:T(8,128)(2,1)S(1)} %bitcast.10, bf16[2,264,268]{2,1,0:T(8,128)(2,1)S(1)} %get-tuple-element.22.w_ref, f32[1,128]{1,0:T(1,128)S(1)} %get-tuple-element.23.xs_ref, f32[264]{0:T(512)S(1)} %get-tuple-element.24.ys_ref), custom_call_target="tpu_custom_call" | custom-call | flops 100000000 | bytes 1099680 | tf_op jit(solution)/shard_map/y_partial/pallas_call | solution.py:361
  14.7 0.0 copy-start.1
  14.7 7.6 %all-to-all-done.c_ref = bf16[32,8,128]{2,1,0:T(8,128)(2,1)S(1)} async-done(((bf16[32,8,128]{2,1,0:T(8,128)(2,1)}), bf16[32,8,128]{2,1,0:T(8,128)(2,1)S(1)}, u32[]{:S(2)}, u32[]{:S(2)}) %all-to-all-start) | async-done | bytes 65568 | tf_op jit(solution)/shard_map/all_to_all | solution.py:402
  22.3 12.4 %all-to-all-start.1 = ((bf16[16,56,128]{2,1,0:T(8,128)(2,1)}), bf16[16,56,128]{2,1,0:T(8,128)(2,1)S(1)}, u32[]{:S(2)}, u32[]{:S(2)}) async-start(bf16[16,56,128]{2,1,0:T(8,128)(2,1)} %y_partial.1.after_ref), calls=%async_computation.1 | async-start | bytes 458752 | tf_op jit(solution)/shard_map/all_to_all | solution.py:409
  34.8 0.0 copy-done.5
  34.8 0.0 copy-start.2
  34.8 0.0 copy-done.6
  34.8 0.0 copy-done.3
  34.9 0.0 copy-done.4
  34.9 2.0 %own.1 = (f32[12,264,128]{2,1,0:T(8,128)S(1)}, bf16[16,256]{1,0:T(8,128)(2,1)S(1)}, bf16[2,16,264]{2,1,0:T(8,128)(2,1)S(1)}, f32[8,128]{1,0:T(8,128)S(1)}, f32[8,384]{1,0:T(8,128)S(1)}) custom-call(s32[8,128]{1,0:T(8,128)S(1)} %get-tuple-element.18.count_ref, bf16[12,264,128]{2,1,0:T(8,128)(2,1)S(1)} %bitcast.11, ...), custom_call_target="tpu_custom_call" | custom-call | flops 600000000 | bytes 1410752 | tf_op jit(solution)/shard_map/own/pallas_call | solution.py:361
  36.9 0.0 copy-done.1
  36.9 0.3 x_solve.1.s_ref
  37.2 8.6 %all-to-all-done.1.r_ref = bf16[16,56,128]{2,1,0:T(8,128)(2,1)S(1)} async-done(((bf16[16,56,128]{2,1,0:T(8,128)(2,1)}), bf16[16,56,128]{2,1,0:T(8,128)(2,1)S(1)}, u32[]{:S(2)}, u32[]{:S(2)}) %all-to-all-start.1) | async-done | bytes 229408 | tf_op jit(solution)/shard_map/all_to_all | solution.py:409
  45.8 0.7 %top.1 = bf16[32,8,128]{2,1,0:T(8,128)(2,1)} custom-call(bf16[32,8,128]{2,1,0:T(8,128)(2,1)S(1)} %x_solve.1.s_ref, bf16[16,56,128]{2,1,0:T(8,128)(2,1)S(1)} %all-to-all-done.1.r_ref, f32[8,128]{1,0:T(8,128)S(1)} %get-tuple-element.25.after_ref.xx_ref), custom_call_target="tpu_custom_call" | custom-call | bytes 299008 | tf_op jit(solution)/shard_map/top/pallas_call | solution.py:361
  46.5 3.9 %all-to-all-start.2 = ((bf16[32,8,128]{2,1,0:T(8,128)(2,1)}), bf16[32,8,128]{2,1,0:T(8,128)(2,1)S(1)}, u32[]{:S(2)}, u32[]{:S(2)}) async-start(bf16[32,8,128]{2,1,0:T(8,128)(2,1)} %top.1), calls=%async_computation.2 | async-start | bytes 131072 | tf_op jit(solution)/shard_map/all_to_all | solution.py:429
  50.4 0.0 copy-done.2
  50.4 0.5 y_solve.1
  50.8 1.9 %collective-permute-start = (bf16[8,768]{1,0:T(8,128)(2,1)S(1)}, bf16[8,768]{1,0:T(8,128)(2,1)S(1)}, u32[]{:S(2)}, u32[]{:S(2)}) collective-permute-start(bf16[8,768]{1,0:T(8,128)(2,1)S(1)} %get-tuple-element.26), channel_id=1, source_target_pairs={{0,32},{32,0},{1,33},{33,1},{2,34},{34,2},{3,35},{35,3},{4,36},{36... | collective-permute-start | bytes 36872 | tf_op jit(solution)/shard_map/ppermute | solution.py:437
  52.8 0.6 y_add.2.own_ref
  53.4 0.0 copy-start
  53.4 0.5 collective-permute-done.coef_ref
  53.9 0.6 y_add.3.base_ref
  54.5 5.6 %all-to-all-done.2.c_ref = bf16[32,8,128]{2,1,0:T(8,128)(2,1)S(1)} async-done(((bf16[32,8,128]{2,1,0:T(8,128)(2,1)}), bf16[32,8,128]{2,1,0:T(8,128)(2,1)S(1)}, u32[]{:S(2)}, u32[]{:S(2)}) %all-to-all-start.2) | async-done | bytes 65568 | tf_op jit(solution)/shard_map/all_to_all | solution.py:429
  60.1 0.0 copy-done
  60.1 1.9 %finish.1 = (bf16[12,264,128]{2,1,0:T(8,128)(2,1)}, bf16[12,264,128]{2,1,0:T(8,128)(2,1)}) custom-call(s32[8,128]{1,0:T(8,128)S(1)} %get-tuple-element.18.count_ref, bf16[32,8,128]{2,1,0:T(8,128)(2,1)S(1)} %all-to-all-done.2.c_ref, bf16[12,264,128]{2,1,0:T(8,128)(2,1)S(1)} %bitcast.14, bf16[12,264,128]{2,1,0:T(8,128)(2,1)S(1)} %bitcast.15, ...), custom_call_target="tpu_custom_call" | custom-call | flops 100000000 | bytes 3325952 | tf_op jit(solution)/shard_map/finish/pallas_call | solution.py:361
  (3 shorter events, 0.0 us)
Async XLA Ops:
  0.6 34.1 %copy-start.5 = (f32[1,2,2,264]{3,2,1,0:T(2,128)S(1)}, f32[1,2,2,264]{3,2,1,0:T(2,128)}, u32[]{:S(2)}) copy-start(f32[1,2,2,264]{3,2,1,0:T(2,128)} %param.25) | copy-start | bytes 12676
  0.6 34.2 %copy-start.6 = (f32[2,2,128]{2,1,0:T(2,128)S(1)}, f32[2,2,128]{2,1,0:T(2,128)}, u32[]{:S(2)}) copy-start(f32[2,2,128]{2,1,0:T(2,128)} %param.22) | copy-start | bytes 6148
  0.7 34.2 %copy-start.3 = (f32[264]{0:T(512)S(1)}, f32[264]{0:T(512)}, u32[]{:S(2)}) copy-start(f32[264]{0:T(512)} %yc_ref.1) | copy-start | bytes 3172
  0.7 34.2 %copy-start.4 = (f32[128]{0:T(128)S(1)}, f32[128]{0:T(128)}, u32[]{:S(2)}) copy-start(f32[128]{0:T(128)} %param.17) | copy-start | bytes 1540
  3.0 19.3 %all-to-all-start = ((bf16[32,8,128]{2,1,0:T(8,128)(2,1)}), bf16[32,8,128]{2,1,0:T(8,128)(2,1)S(1)}, u32[]{:S(2)}, u32[]{:S(2)}) async-start(bf16[32,8,128]{2,1,0:T(8,128)(2,1)} %get-tuple-element.19), calls=%async_computation | async-start | bytes 131072 | tf_op jit(solution)/shard_map/all_to_all | solution.py:402
  14.7 22.1 %copy-start.1 = (f32[2,64,64]{2,1,0:T(8,128)S(1)}, f32[2,64,64]{2,1,0:T(8,128)}, u32[]{:S(2)}) copy-start(f32[2,64,64]{2,1,0:T(8,128)} %coupling_ref.2) | copy-start | bytes 98308
  22.3 23.5 %all-to-all-start.1 = ((bf16[16,56,128]{2,1,0:T(8,128)(2,1)}), bf16[16,56,128]{2,1,0:T(8,128)(2,1)S(1)}, u32[]{:S(2)}, u32[]{:S(2)}) async-start(bf16[16,56,128]{2,1,0:T(8,128)(2,1)} %y_partial.1.after_ref), calls=%async_computation.1 | async-start | bytes 458752 | tf_op jit(solution)/shard_map/all_to_all | solution.py:409
  34.8 15.6 %copy-start.2 = (f32[2,32,32]{2,1,0:T(8,128)S(1)}, f32[2,32,32]{2,1,0:T(8,128)}, u32[]{:S(2)}) copy-start(f32[2,32,32]{2,1,0:T(8,128)} %coupling_ref.3) | copy-start | bytes 24580
  46.5 13.6 %all-to-all-start.2 = ((bf16[32,8,128]{2,1,0:T(8,128)(2,1)}), bf16[32,8,128]{2,1,0:T(8,128)(2,1)S(1)}, u32[]{:S(2)}, u32[]{:S(2)}) async-start(bf16[32,8,128]{2,1,0:T(8,128)(2,1)} %top.1), calls=%async_computation.2 | async-start | bytes 131072 | tf_op jit(solution)/shard_map/all_to_all | solution.py:429
  50.8 3.1 %collective-permute-start = (bf16[8,768]{1,0:T(8,128)(2,1)S(1)}, bf16[8,768]{1,0:T(8,128)(2,1)S(1)}, u32[]{:S(2)}, u32[]{:S(2)}) collective-permute-start(bf16[8,768]{1,0:T(8,128)(2,1)S(1)} %get-tuple-element.26), channel_id=1, source_target_pairs={{0,32},{32,0},{1,33},{33,1},{2,34},{34,2},{3,35},{35,3},{4,36},{36... | collective-permute-start | bytes 36872 | tf_op jit(solution)/shard_map/ppermute | solution.py:437
  53.4 6.7 %copy-start = (bf16[3,4,264,128]{3,2,1,0:T(8,128)(2,1)S(1)}, bf16[3,4,264,128]{3,2,1,0:T(8,128)(2,1)}, u32[]{:S(2)}) copy-start(bf16[3,4,264,128]{3,2,1,0:T(8,128)(2,1)} %param.14) | copy-start | bytes 2433028

commit v4 on v3

--- a/solution.py
+++ b/solution.py
@@ -1,5 +1,3 @@
-import functools
-
 import jax
 import jax.numpy as jnp
 from jax import lax
@@ -26,8 +24,7 @@
 LINES = NP * YR
 CHUNK = 112
 CHUNKS = -(-LINES // CHUNK)
-HALF = NP // 2
-TILES = HALF + 1
+TILES = NP + 1
 GROUP = 4
 EDGE_X = (0, 1, XW - 2, XW - 1)
 HALO_X = (0, 1, XW + 2, XW + 3)
@@ -156,14 +153,16 @@
     top = jnp.where(live, top, F32(0.0))
     top = jnp.max(jnp.max(top, axis=0, keepdims=True), axis=1, keepdims=True)
     last = jnp.where(row8 < 4, margin, pltpu.roll(max_tile(top), 4, 0))
-    for half in range(2):
-        tiles = [nn(weights, v_ref[HALF * half + g]) for g in range(HALF)]
-        whole = jnp.concatenate(tiles + [last], axis=0).astype(BF16)
-        for chip in range(NROW // 2):
-            o_ref[2 * chip + half] = whole
-
-
-def x_solve_kernel(c_ref, x_ref, coupling_ref, o_ref, a_ref, e_ref, s_ref):
+    tiles = [nn(weights, v_ref[p]) for p in range(NP)]
+    o_ref[0] = jnp.concatenate(tiles + [last], axis=0).astype(BF16)
+
+
+def top_of(ref, first, count, stride):
+    parts = [ref[pl.ds(first + j, count, stride=stride), :] for j in range(3)]
+    return jnp.max(parts[0] + parts[1] + parts[2], axis=0, keepdims=True)
+
+
+def x_solve_kernel(c_ref, x_ref, coupling_ref, r_ref, o_ref, a_ref, e_ref, s_ref, t_ref):
     a_ref[...] = c_ref[...].astype(F32).reshape(NCOL * 8, 128)
     part = [a_ref[pl.ds(v, NCOL, stride=8), :] for v in range(8)]
     margin = [pltpu.roll(part[6], 1, 0), pltpu.roll(part[7], 1, 0)]
@@ -182,34 +181,26 @@
             a_ref[pl.ds(2 * k + e, NCOL, stride=8), :] = s_ref[k, pl.ds(e, NCOL, stride=2), :]
     for h in range(4):
         a_ref[pl.ds(4 + h, NCOL, stride=8), :] = margin[h]
-    o_ref[...] = a_ref[...].reshape(NCOL, 8, 128).astype(BF16)
-
-
-def top_of(ref, first, count, stride):
-    parts = [ref[pl.ds(first + j, count, stride=stride), :] for j in range(3)]
-    return jnp.max(parts[0] + parts[1] + parts[2], axis=0, keepdims=True)
-
-
-def top_kernel(s_ref, r_ref, after_ref, o_ref, t_ref):
-    t_ref[...] = r_ref[...][:, 8 * HALF : 8 * TILES, :].astype(F32).reshape(8 * NROW, 128)
+    t_ref[...] = r_ref[...][:, 8 * NP : 8 * TILES, :].astype(F32).reshape(8 * NROW, 128)
     tile = max_tile(top_of(t_ref, 4, NROW, 8))
     spare = iota((8, 128), 1) >= CHUNK
-    o_ref[...] = jnp.where(spare[None], tile[None], s_ref[...].astype(F32)).astype(BF16)
-
-
-def y_solve_kernel(r_ref, coupling_ref, keep_ref, send_ref, a_ref, e_ref, s_ref, m_ref):
+    solved = a_ref[...].reshape(NCOL, 8, 128)
+    o_ref[...] = jnp.where(spare[None], tile[None], solved).astype(BF16)
+
+
+def y_solve_kernel(r_ref, coupling_ref, o_ref, a_ref, e_ref, s_ref, m_ref):
     a_ref[...] = r_ref[...].astype(F32).reshape(NROW * 8 * TILES, 128)
 
     def rows_of(place):
         return a_ref[pl.ds(place, NROW, stride=8 * TILES), :]
 
     source = iota((NROW, 128), 0)
-    weights = [rows_of(8 * HALF + j) for j in range(4)]
+    weights = [rows_of(8 * NP + j) for j in range(4)]
     weight = [
         [jnp.broadcast_to(weights[j][:, h : h + 1], (NROW, 128)) for h in range(4)]
         for j in range(4)
     ]
-    for g in range(HALF):
+    for g in range(NP):
         lanes = slice(128 * g, 128 * g + 128)
         part = [rows_of(8 * g + v) for v in range(8)]
         margin = [pltpu.roll(part[6 + h], 1, 0) for h in range(2)]
@@ -223,16 +214,14 @@
                 ends = part[2 * k + e]
                 for h in range(4):
                     ends = ends + weight[2 * k + e][h] * margin[h]
-                e_ref[HALF * k + g, pl.ds(e, NROW, stride=2), :] = ends
+                e_ref[NP * k + g, pl.ds(e, NROW, stride=2), :] = ends
     for k in range(2):
-        ends = jnp.concatenate([e_ref[HALF * k + g] for g in range(HALF)], axis=1)
+        ends = jnp.concatenate([e_ref[NP * k + g] for g in range(NP)], axis=1)
         s_ref[k] = nn(coupling_ref[k], ends, lax.Precision.HIGHEST)
-    core = lax.axis_index("row_1")
     own = row_pos()
-    for block, out in ((own, keep_ref), (own + 1 - 2 * core, send_ref)):
-        pieces = [s_ref[k, pl.ds(2 * block + e, 1), :] for k in range(2) for e in range(2)]
-        pieces += [m_ref[h, pl.ds(block, 1), :] for h in range(4)]
-        out[...] = jnp.concatenate(pieces, axis=0).astype(BF16)
+    pieces = [s_ref[k, pl.ds(2 * own + e, 1), :] for k in range(2) for e in range(2)]
+    pieces += [m_ref[h, pl.ds(own, 1), :] for h in range(4)]
+    o_ref[...] = jnp.concatenate(pieces, axis=0).astype(BF16)
 
 
 def own_kernel(
@@ -295,18 +284,16 @@
                 own_ref[p] = rhs + y_second * of_second[:, at]
 
 
-def y_add_kernel(other, coef_ref, v_ref, own_ref, hc_ref, yy_ref, o_ref):
-    core = lax.axis_index("row_1")
-    half = 1 - core if other else core
+def y_add_kernel(coef_ref, v_ref, own_ref, hc_ref, yy_ref, o_ref):
     scale, curv, y_second = (column_tiles(yy_ref, j) for j in range(3))
-    for g in range(0, HALF, 2):
-        coef = coef_ref[:, 128 * g : 128 * g + 256].astype(F32)
+    for pair in range(0, NP, 2):
+        coef = coef_ref[:, 128 * pair : 128 * pair + 256].astype(F32)
         coef = jnp.concatenate([coef, coef], axis=0).astype(BF16)
         of_first, of_second = tn(hc_ref[0], coef), tn(hc_ref[1], coef)
         for j in range(2):
-            p = HALF * half + g + j
+            p = pair + j
             at = slice(128 * j, 128 * j + 128)
-            v = v_ref[4 + lax.rem(p, 4)].astype(F32)
+            v = v_ref[4 + p % 4].astype(F32)
             add = (curv - v * scale) * of_first[:, at] + y_second * of_second[:, at]
             o_ref[p] = own_ref[p] + add
 
@@ -402,19 +389,22 @@
     theirs = lax.all_to_all(mine, COL, 0, 0, tiled=True)
     y_part = call(
         y_partial_kernel, "y_partial", (count, planes, y_mats, x_scale, y_scale),
-        (shape((NROW, 8 * TILES, 128)),), ((16, 384),), flops=10**8,
-    )
+        (shape((1, 8 * TILES, 128)),), ((16, 384),), flops=10**8,
+    )
+    columns = lax.all_gather(y_part, ROW, axis=0, tiled=True)
     x_basis = jnp.pad(x_basis.reshape(4, XW), ((0, 4), (0, 0)))
     y_basis = jnp.pad(y_basis.reshape(4, YR), ((0, 4), (0, 0)))
-    columns = lax.all_to_all(y_part, ROW, 0, 0, tiled=True)
     x_solved = call(
-        x_solve_kernel, "x_solve", (theirs, x_rows, x_coupling), (shape((NCOL, 8, 128)),),
-        ((NCOL * 8, 128), (2, 2 * NCOL, 128), (2, 2 * NCOL, 128)), flops=10**8,
-    )
+        x_solve_kernel, "x_solve", (theirs, x_rows, x_coupling, columns), (shape((NCOL, 8, 128)),),
+        ((NCOL * 8, 128), (2, 2 * NCOL, 128), (2, 2 * NCOL, 128), (8 * NROW, 128)), flops=10**8,
+    )
+    x_back = lax.all_to_all(x_solved, COL, 0, 0, tiled=True)
     own, x_corr, y_corr, x_lines, y_lines = call(
         own_kernel, "own",
-        (count, planes, x_rows, x_basis, y_mats, y_basis, x_scale, x_curv, y_scale, y_curv,
-            y_part),
+        (
+            count, planes, x_rows, x_basis, y_mats, y_basis, x_scale, x_curv, y_scale, y_curv,
+            x_solved,
+        ),
         (
             shape((NP, YR, XW), F32), shape((16, 2 * XW)), shape((2, 16, YR)),
             shape((8, XW), F32), shape((8, 384), F32),
@@ -422,26 +412,17 @@
         (pltpu.VMEM((XW, 2 * XW), BF16), pltpu.VMEM((2, YR, YR), BF16)),
         flops=6 * 10**8, mib=8, far=(10,),
     )
-    x_back = call(
-        top_kernel, "top", (x_solved, columns, x_lines), (shape((NCOL, 8, 128)),),
-        ((8 * NROW, 128),), far=(2,),
-    )
-    x_back = lax.all_to_all(x_back, COL, 0, 0, tiled=True)
-    wide = 128 * HALF
-    keep, send = call(
-        y_solve_kernel, "y_solve", (columns, y_coupling), (shape((8, wide)), shape((8, wide))),
+    wide = 128 * NP
+    y_solved = call(
+        y_solve_kernel, "y_solve", (columns, y_coupling), (shape((8, wide)),),
         (
-            (NROW * 8 * TILES, 128), (NP, 2 * NROW, 128), (2, 2 * NROW, wide), (4, NROW, wide),
+            (NROW * 8 * TILES, 128), (2 * NP, 2 * NROW, 128), (2, 2 * NROW, wide), (4, NROW, wide),
         ), flops=10**8,
     )
-    got = lax.ppermute(send, "row_1", [(0, 1), (1, 0)])
-    base = own
-    for other, coefs in enumerate((keep, got)):
-        base = call(
-            functools.partial(y_add_kernel, other), "y_add",
-            (coefs, planes, base, y_corr, y_lines),
-            (shape(own.shape, F32),), flops=10**8, alias={2: 0},
-        )
+    base = call(
+        y_add_kernel, "y_add", (y_solved, planes, own, y_corr, y_lines),
+        (shape(own.shape, F32),), flops=10**8, alias={2: 0},
+    )
     rhs, inc = call(
         finish_kernel, "finish",
         (count, x_back, planes, previous, base, x_corr, x_lines),

time: 62.3 us -> 60.9 us (0.978)
  blocking collectives: 0 us -> 25.1 us
  waiting for transfers between devices: 22.3 us -> 4.93 us
  starting transfers between devices: 28.7 us -> 20.1 us
    all_gather x0 -> x1, blocking collectives: none -> 25.1 us  [shards(): columns = lax.all_gather(y_part, ROW, axis=0, tiled=True)]
    all_to_all x2 -> x1, waiting for transfers between devices: 14.1 us -> 4.93 us  [shards(): x_back = lax.all_to_all(x_solved, COL, 0, 0, tiled=True)]
    all_to_all x1, waiting for transfers between devices: 7.6 us -> 0.01 us  [shards(): theirs = lax.all_to_all(mine, COL, 0, 0, tiled=True)]
    all_to_all x2 -> x1, starting transfers between devices: 16.3 us -> 9.49 us  [shards(): x_back = lax.all_to_all(x_solved, COL, 0, 0, tiled=True)]
    ppermute x1 -> x0, starting transfers between devices: 1.92 us -> none  [shards(): got = lax.ppermute(send, 'row_1', [(0, 1), (1, 0)])]
    pallas_call x9 -> x7, Pallas kernels: 10.1 us -> 9.52 us  [call(): pl.pallas_call(body, out_shape=outs[0] if single else outs, in_specs=spec...]
  transfers between devices with their start and end apart: 4 -> 2, of which waited for: 4 -> 1; matrix products, arithmetic and copies ran while one was open for 0% -> 0% of each run, Pallas kernels for 8% -> 7%
where the time goes in v4:
time: 60.9 us; the launch traced here: 60.6 us
  blocking collectives  25.1 us (41%)
  starting transfers between devices  20.1 us (33%)
  Pallas kernels  9.52 us (16%)
  waiting for transfers between devices  4.93 us (8%)
  between operations  0.8 us (1%)
    all_gather x1, blocking collectives, shards(): columns = lax.all_gather(y_part, ROW, axis=0, tiled=True)  25.1 us
    all_to_all x1, starting transfers between devices, shards(): theirs = lax.all_to_all(mine, COL, 0, 0, tiled=True)  10.6 us
    pallas_call x7, Pallas kernels, call(): pl.pallas_call(body, out_shape=outs[0] if single else outs, in_specs=spec...  9.52 us
    all_to_all x1, starting transfers between devices, shards(): x_back = lax.all_to_all(x_solved, COL, 0, 0, tiled=True)  9.49 us
    all_to_all x1, waiting for transfers between devices, shards(): x_back = lax.all_to_all(x_solved, COL, 0, 0, tiled=True)  4.93 us
  transfers between devices with their start and end apart: 2, of which 1 were waited for; matrix products, arithmetic and copies ran while one was open for 0% of the time, Pallas kernels for 7%

profile of v4, /device:TPU:1, one launch (start us, length us, event | category | flops | bytes accessed | tf_op | source)
XLA Modules:
  0.0 60.6 jit_solution(3993146916871728230)
XLA Ops:
  0.6 0.0 copy-start.1
  0.6 2.3 %x_partial.1 = (bf16[32,8,128]{2,1,0:T(8,128)(2,1)}, bf16[3168,128]{1,0:T(8,128)(2,1)S(1)}, bf16[264,128]{1,0:T(8,128)(2,1)S(1)}, bf16[2,264,268]{2,1,0:T(8,128)...) custom-call(bf16[3168,128]{1,0:T(8,128)(2,1)} %bitcast.16, bf16[264,128]{1,0:T(8,128)(2,1)} %bitcast.18, ...), custom_call_target="tpu_custom_call" | custom-call | flops 100000000 | bytes 1163232 | tf_op jit(solution)/shard_map/x_partial/pallas_call | solution.py:348
  3.0 0.0 copy-start.5
  3.0 0.0 copy-start.6
  3.0 0.0 copy-start.2
  3.0 0.0 copy-start.3
  3.0 0.0 copy-start.4
  3.0 10.6 %all-to-all-start = ((bf16[32,8,128]{2,1,0:T(8,128)(2,1)}), bf16[32,8,128]{2,1,0:T(8,128)(2,1)S(1)}, u32[]{:S(2)}, u32[]{:S(2)}) async-start(bf16[32,8,128]{2,1,0:T(8,128)(2,1)} %get-tuple-element.17), calls=%async_computation | async-start | bytes 131072 | tf_op jit(solution)/shard_map/all_to_all | solution.py:389
  13.7 0.5 y_partial.1
  14.2 25.1 %all_gather.3.r_ref = bf16[16,104,128]{2,1,0:T(8,128)(2,1)S(1)} all-gather(bf16[1,104,128]{2,1,0:T(8,128)(2,1)S(1)} %y_partial.1), channel_id=1, replica_groups=mesh['row_0'=8,'row_1'=2,'col_0'=8,'col_1'=4] {'row_0','row_1'}, dimensions={0}, use_global_device_ids=true | all-gather | bytes 452608 | tf_op jit(solution)/shard_map/all_gather | solution.py:394
  39.3 0.0 all-to-all-done.c_ref
  39.3 0.0 copy-done.1
  39.3 1.0 %x_solve.1.after_ref = bf16[32,8,128]{2,1,0:T(8,128)(2,1)} custom-call(bf16[32,8,128]{2,1,0:T(8,128)(2,1)S(1)} %all-to-all-done.c_ref, bf16[264,128]{1,0:T(8,128)(2,1)S(1)} %get-tuple-element.18.x_ref, f32[2,64,64]{2,1,0:T(8,128)S(1)} %copy-done.1, bf16[16,104,128]{2,1,0:T(8,128)(2,1)S(1)} %all_gather.3.r_ref), custom_call_target="tpu_custom_call" | custom-call | flops 100000000 | bytes 591872 | tf_op jit(solution)/shard_map/x_solve/pallas_call | solution.py:348
  40.3 9.5 %all-to-all-start.1 = ((bf16[32,8,128]{2,1,0:T(8,128)(2,1)}), bf16[32,8,128]{2,1,0:T(8,128)(2,1)S(1)}, u32[]{:S(2)}, u32[]{:S(2)}) async-start(bf16[32,8,128]{2,1,0:T(8,128)(2,1)} %x_solve.1.after_ref), calls=%async_computation.1 | async-start | bytes 131072 | tf_op jit(solution)/shard_map/all_to_all | solution.py:401
  49.8 0.0 copy-done.5
  49.8 0.0 copy-done.6
  49.9 0.0 copy-done.2
  49.9 0.7 %y_solve.1.coef_ref = bf16[8,1536]{1,0:T(8,128)(2,1)S(1)} custom-call(bf16[16,104,128]{2,1,0:T(8,128)(2,1)S(1)} %all_gather.3.r_ref, f32[2,32,32]{2,1,0:T(8,128)S(1)} %copy-done.2), custom_call_target="tpu_custom_call" | custom-call | flops 100000000 | bytes 434176 | tf_op jit(solution)/shard_map/y_solve/pallas_call | solution.py:348
  50.6 0.0 copy-done.3
  50.6 0.0 copy-done.4
  50.6 2.0 %own.1 = (f32[12,264,128]{2,1,0:T(8,128)S(1)}, bf16[16,256]{1,0:T(8,128)(2,1)S(1)}, bf16[2,16,264]{2,1,0:T(8,128)(2,1)S(1)}, f32[8,128]{1,0:T(8,128)S(1)}, f32[8,384]{1,0:T(8,128)S(1)}) custom-call(s32[8,128]{1,0:T(8,128)S(1)} %get-tuple-element.16.count_ref, bf16[12,264,128]{2,1,0:T(8,128)(2,1)S(1)} %bitcast.11, ...), custom_call_target="tpu_custom_call" | custom-call | flops 600000000 | bytes 1246912 | tf_op jit(solution)/shard_map/own/pallas_call | solution.py:348
  52.6 0.0 copy-start
  52.6 1.1 %y_add.1.base_ref = f32[12,264,128]{2,1,0:T(8,128)S(1)} custom-call(bf16[8,1536]{1,0:T(8,128)(2,1)S(1)} %y_solve.1.coef_ref, bf16[12,264,128]{2,1,0:T(8,128)(2,1)S(1)} %bitcast.12, f32[12,264,128]{2,1,0:T(8,128)S(1)} %get-tuple-element.23.own_ref, bf16[2,16,264]{2,1,0:T(8,128)(2,1)S(1)} %get-tuple-element.24.hc_ref, ...), custom_call_target="tpu_custom_call", output_to_operand_aliasing={{}: (2, {})} | custom-call | flops 100000000 | bytes 2486784 | tf_op jit(solution)/shard_map/y_add/pallas_call | solution.py:348
  53.7 4.9 %all-to-all-done.1.c_ref = bf16[32,8,128]{2,1,0:T(8,128)(2,1)S(1)} async-done(((bf16[32,8,128]{2,1,0:T(8,128)(2,1)}), bf16[32,8,128]{2,1,0:T(8,128)(2,1)S(1)}, u32[]{:S(2)}, u32[]{:S(2)}) %all-to-all-start.1) | async-done | bytes 65568 | tf_op jit(solution)/shard_map/all_to_all | solution.py:401
  58.7 0.0 copy-done
  58.7 1.9 %finish.1 = (bf16[12,264,128]{2,1,0:T(8,128)(2,1)}, bf16[12,264,128]{2,1,0:T(8,128)(2,1)}) custom-call(s32[8,128]{1,0:T(8,128)S(1)} %get-tuple-element.16.count_ref, bf16[32,8,128]{2,1,0:T(8,128)(2,1)S(1)} %all-to-all-done.1.c_ref, bf16[12,264,128]{2,1,0:T(8,128)(2,1)S(1)} %bitcast.13, bf16[12,264,128]{2,1,0:T(8,128)(2,1)S(1)} %bitcast.14, ...), custom_call_target="tpu_custom_call" | custom-call | flops 100000000 | bytes 3325952 | tf_op jit(solution)/shard_map/finish/pallas_call | solution.py:348
  (3 shorter events, 0.0 us)
Async XLA Ops:
  0.6 38.7 %copy-start.1 = (f32[2,64,64]{2,1,0:T(8,128)S(1)}, f32[2,64,64]{2,1,0:T(8,128)}, u32[]{:S(2)}) copy-start(f32[2,64,64]{2,1,0:T(8,128)} %coupling_ref.2) | copy-start | bytes 98308
  3.0 46.8 %copy-start.5 = (f32[1,2,2,264]{3,2,1,0:T(2,128)S(1)}, f32[1,2,2,264]{3,2,1,0:T(2,128)}, u32[]{:S(2)}) copy-start(f32[1,2,2,264]{3,2,1,0:T(2,128)} %param.25) | copy-start | bytes 12676
  3.0 46.8 %copy-start.6 = (f32[2,2,128]{2,1,0:T(2,128)S(1)}, f32[2,2,128]{2,1,0:T(2,128)}, u32[]{:S(2)}) copy-start(f32[2,2,128]{2,1,0:T(2,128)} %param.22) | copy-start | bytes 6148
  3.0 46.9 %copy-start.2 = (f32[2,32,32]{2,1,0:T(8,128)S(1)}, f32[2,32,32]{2,1,0:T(8,128)}, u32[]{:S(2)}) copy-start(f32[2,32,32]{2,1,0:T(8,128)} %coupling_ref.3) | copy-start | bytes 24580
  3.0 47.6 %copy-start.3 = (f32[264]{0:T(512)S(1)}, f32[264]{0:T(512)}, u32[]{:S(2)}) copy-start(f32[264]{0:T(512)} %yc_ref.1) | copy-start | bytes 3172
  3.0 47.6 %copy-start.4 = (f32[128]{0:T(128)S(1)}, f32[128]{0:T(128)}, u32[]{:S(2)}) copy-start(f32[128]{0:T(128)} %param.17) | copy-start | bytes 1540
  3.0 36.3 %all-to-all-start = ((bf16[32,8,128]{2,1,0:T(8,128)(2,1)}), bf16[32,8,128]{2,1,0:T(8,128)(2,1)S(1)}, u32[]{:S(2)}, u32[]{:S(2)}) async-start(bf16[32,8,128]{2,1,0:T(8,128)(2,1)} %get-tuple-element.17), calls=%async_computation | async-start | bytes 131072 | tf_op jit(solution)/shard_map/all_to_all | solution.py:389
  40.3 18.4 %all-to-all-start.1 = ((bf16[32,8,128]{2,1,0:T(8,128)(2,1)}), bf16[32,8,128]{2,1,0:T(8,128)(2,1)S(1)}, u32[]{:S(2)}, u32[]{:S(2)}) async-start(bf16[32,8,128]{2,1,0:T(8,128)(2,1)} %x_solve.1.after_ref), calls=%async_computation.1 | async-start | bytes 131072 | tf_op jit(solution)/shard_map/all_to_all | solution.py:401
  52.6 6.0 %copy-start = (bf16[3,4,264,128]{3,2,1,0:T(8,128)(2,1)S(1)}, bf16[3,4,264,128]{3,2,1,0:T(8,128)(2,1)}, u32[]{:S(2)}) copy-start(bf16[3,4,264,128]{3,2,1,0:T(8,128)(2,1)} %param.14) | copy-start | bytes 2433028

commit v5 on v4

--- a/solution.py
+++ b/solution.py
@@ -225,9 +225,11 @@
 
 
 def own_kernel(
-    count_ref, v_ref, x_ref, xb_ref, w_ref, yb_ref, xs_ref, xv_ref, ys_ref, yc_ref,
-    after_ref, own_ref, xc_ref, hc_ref, xx_ref, yy_ref, xo_ref, wm_ref,
+    count_ref, v_hbm, x_ref, xb_ref, w_ref, yb_ref, xs_ref, xv_ref, ys_ref, yc_ref,
+    coef_ref, after_ref, own_ref, xc_ref, xx_ref, u_ref, hc_ref, yy_ref, xo_ref, wm_ref, v_ref, sem,
 ):
+    fetch = pltpu.make_async_copy(v_hbm, v_ref, sem.at[0])
+    fetch.start()
     count = count_ref[0:1, 0:1]
     x_all = x_ref[...]
     n_in = 2 * (XW + 4)
@@ -269,11 +271,17 @@
     xs, xv = xs_ref[...], viscosity * xv_ref[...]
     x_second = viscosity * xs * xs
     xx_ref[...] = jnp.concatenate([xs, xv, x_second, jnp.zeros((5, XW), F32)], axis=0)
+    fetch.wait()
+    for z in range(4):
+        u_ref[z] = v_ref[z]
     for pair in range(2):
         for f in range(3):
             plane = 4 * f + 2 * pair
             both = jnp.concatenate([v_ref[plane], v_ref[plane + 1]], axis=1)
-            of_first, of_second = nn(wm_ref[0], both), nn(wm_ref[1], both)
+            coef = coef_ref[:, XW * plane : XW * plane + 2 * XW].astype(F32)
+            coef = jnp.concatenate([coef, coef], axis=0).astype(BF16)
+            of_first = nn(wm_ref[0], both) + tn(hc_ref[0], coef)
+            of_second = nn(wm_ref[1], both) + tn(hc_ref[1], coef)
             for j in range(2):
                 p, z = plane + j, 2 * pair + j
                 at = slice(XW * j, XW * j + XW)
@@ -282,20 +290,6 @@
                 rhs = (xv - u * xs) * in_x[:, 0:XW] + x_second * in_x[:, XW:]
                 rhs = rhs + (curv - v * scale) * of_first[:, at]
                 own_ref[p] = rhs + y_second * of_second[:, at]
-
-
-def y_add_kernel(coef_ref, v_ref, own_ref, hc_ref, yy_ref, o_ref):
-    scale, curv, y_second = (column_tiles(yy_ref, j) for j in range(3))
-    for pair in range(0, NP, 2):
-        coef = coef_ref[:, 128 * pair : 128 * pair + 256].astype(F32)
-        coef = jnp.concatenate([coef, coef], axis=0).astype(BF16)
-        of_first, of_second = tn(hc_ref[0], coef), tn(hc_ref[1], coef)
-        for j in range(2):
-            p = pair + j
-            at = slice(128 * j, 128 * j + 128)
-            v = v_ref[4 + p % 4].astype(F32)
-            add = (curv - v * scale) * of_first[:, at] + y_second * of_second[:, at]
-            o_ref[p] = own_ref[p] + add
 
 
 def finish_kernel(
@@ -372,6 +366,7 @@
     y_mats = jnp.transpose(y_local, (1, 2, 0))
     x_scale, x_curv = x_scale.reshape(1, XW), x_curv.reshape(1, XW)
 
+    whole = pltpu.with_memory_space_constraint(velocity.reshape(NP, YR, XW), pltpu.HBM)
     fetched = (lines, x_rows, y_mats, x_scale, y_scale)
     *fetched, row_counts = [
         pltpu.with_memory_space_constraint(item, pltpu.HBM) for item in (*fetched, row_counts)
@@ -399,19 +394,6 @@
         ((NCOL * 8, 128), (2, 2 * NCOL, 128), (2, 2 * NCOL, 128), (8 * NROW, 128)), flops=10**8,
     )
     x_back = lax.all_to_all(x_solved, COL, 0, 0, tiled=True)
-    own, x_corr, y_corr, x_lines, y_lines = call(
-        own_kernel, "own",
-        (
-            count, planes, x_rows, x_basis, y_mats, y_basis, x_scale, x_curv, y_scale, y_curv,
-            x_solved,
-        ),
-        (
-            shape((NP, YR, XW), F32), shape((16, 2 * XW)), shape((2, 16, YR)),
-            shape((8, XW), F32), shape((8, 384), F32),
-        ),
-        (pltpu.VMEM((XW, 2 * XW), BF16), pltpu.VMEM((2, YR, YR), BF16)),
-        flops=6 * 10**8, mib=8, far=(10,),
-    )
     wide = 128 * NP
     y_solved = call(
         y_solve_kernel, "y_solve", (columns, y_coupling), (shape((8, wide)),),
@@ -419,13 +401,25 @@
             (NROW * 8 * TILES, 128), (2 * NP, 2 * NROW, 128), (2, 2 * NROW, wide), (4, NROW, wide),
         ), flops=10**8,
     )
-    base = call(
-        y_add_kernel, "y_add", (y_solved, planes, own, y_corr, y_lines),
-        (shape(own.shape, F32),), flops=10**8, alias={2: 0},
+    base, x_corr, x_lines, streamwise = call(
+        own_kernel, "own",
+        (
+            count, whole, x_rows, x_basis, y_mats, y_basis, x_scale, x_curv, y_scale, y_curv,
+            y_solved, x_solved,
+        ),
+        (
+            shape((NP, YR, XW), F32), shape((16, 2 * XW)), shape((8, XW), F32),
+            shape((4, YR, XW)),
+        ),
+        (
+            pltpu.VMEM((2, 16, YR), BF16), (8, 384), pltpu.VMEM((XW, 2 * XW), BF16),
+            pltpu.VMEM((2, YR, YR), BF16), pltpu.VMEM((NP, YR, XW), BF16),
+            pltpu.SemaphoreType.DMA((1,)),
+        ), flops=6 * 10**8, mib=8, far=(1, 11),
     )
     rhs, inc = call(
         finish_kernel, "finish",
-        (count, x_back, planes, previous, base, x_corr, x_lines),
+        (count, x_back, streamwise, previous, base, x_corr, x_lines),
         (shape((NP, YR, XW)), shape((NP, YR, XW))),
         (
             (CHUNK * (CHUNKS - 1) + 128, 2 * XW), (8 * NCOL, 128),

time: 60.9 us -> 60.9 us (level)
    pallas_call x7 -> x6, Pallas kernels: 9.52 us -> 10.1 us  [call(): pl.pallas_call(body, out_shape=outs[0] if single else outs, in_specs=spec...]
  transfers between devices with their start and end apart: 2 -> 2, of which waited for: 1 -> 1; matrix products, arithmetic and copies ran while one was open for 0% -> 0% of each run, Pallas kernels for 7% -> 8%
where the time goes in v5:
time: 60.9 us; the launch traced here: 60.6 us
  blocking collectives  25.1 us (41%)
  starting transfers between devices  20.1 us (33%)
  Pallas kernels  10.1 us (17%)
  waiting for transfers between devices  4.36 us (7%)
  between operations  0.78 us (1%)
    all_gather x1, blocking collectives, shards(): columns = lax.all_gather(y_part, ROW, axis=0, tiled=True)  25.1 us
    all_to_all x1, starting transfers between devices, shards(): theirs = lax.all_to_all(mine, COL, 0, 0, tiled=True)  10.6 us
    pallas_call x6, Pallas kernels, call(): pl.pallas_call(body, out_shape=outs[0] if single else outs, in_specs=spec...  10.1 us
    all_to_all x1, starting transfers between devices, shards(): x_back = lax.all_to_all(x_solved, COL, 0, 0, tiled=True)  9.5 us
    all_to_all x1, waiting for transfers between devices, shards(): x_back = lax.all_to_all(x_solved, COL, 0, 0, tiled=True)  4.36 us
  transfers between devices with their start and end apart: 2, of which 1 were waited for; matrix products, arithmetic and copies ran while one was open for 0% of the time, Pallas kernels for 8%

profile of v5, /device:TPU:1, one launch (start us, length us, event | category | flops | bytes accessed | tf_op | source)
XLA Modules:
  0.0 60.6 jit_solution(4961971493761391636)
XLA Ops:
  0.6 0.0 copy-start.1
  0.6 2.3 %x_partial.1 = (bf16[32,8,128]{2,1,0:T(8,128)(2,1)}, bf16[3168,128]{1,0:T(8,128)(2,1)S(1)}, bf16[264,128]{1,0:T(8,128)(2,1)S(1)}, bf16[2,264,268]{2,1,0:T(8,128)...) custom-call(bf16[3168,128]{1,0:T(8,128)(2,1)} %bitcast.14, bf16[264,128]{1,0:T(8,128)(2,1)} %bitcast.17, ...), custom_call_target="tpu_custom_call" | custom-call | flops 100000000 | bytes 1163232 | tf_op jit(solution)/shard_map/x_partial/pallas_call | solution.py:342
  3.0 0.0 copy-start.5
  3.0 0.0 copy-start.6
  3.0 0.0 copy-start.2
  3.0 0.0 copy-start.3
  3.0 0.0 copy-start.4
  3.0 10.6 %all-to-all-start = ((bf16[32,8,128]{2,1,0:T(8,128)(2,1)}), bf16[32,8,128]{2,1,0:T(8,128)(2,1)S(1)}, u32[]{:S(2)}, u32[]{:S(2)}) async-start(bf16[32,8,128]{2,1,0:T(8,128)(2,1)} %get-tuple-element.16), calls=%async_computation | async-start | bytes 131072 | tf_op jit(solution)/shard_map/all_to_all | solution.py:384
  13.7 0.5 y_partial.1
  14.2 25.1 %all_gather.3.r_ref = bf16[16,104,128]{2,1,0:T(8,128)(2,1)S(1)} all-gather(bf16[1,104,128]{2,1,0:T(8,128)(2,1)S(1)} %y_partial.1), channel_id=1, replica_groups=mesh['row_0'=8,'row_1'=2,'col_0'=8,'col_1'=4] {'row_0','row_1'}, dimensions={0}, use_global_device_ids=true | all-gather | bytes 452608 | tf_op jit(solution)/shard_map/all_gather | solution.py:389
  39.3 0.0 all-to-all-done.c_ref
  39.3 0.0 copy-done.1
  39.3 0.0 copy-start
  39.3 1.0 %x_solve.1.after_ref = bf16[32,8,128]{2,1,0:T(8,128)(2,1)} custom-call(bf16[32,8,128]{2,1,0:T(8,128)(2,1)S(1)} %all-to-all-done.c_ref, bf16[264,128]{1,0:T(8,128)(2,1)S(1)} %get-tuple-element.17.x_ref, f32[2,64,64]{2,1,0:T(8,128)S(1)} %copy-done.1, bf16[16,104,128]{2,1,0:T(8,128)(2,1)S(1)} %all_gather.3.r_ref), custom_call_target="tpu_custom_call" | custom-call | flops 100000000 | bytes 591872 | tf_op jit(solution)/shard_map/x_solve/pallas_call | solution.py:342
  40.3 9.5 %all-to-all-start.1 = ((bf16[32,8,128]{2,1,0:T(8,128)(2,1)}), bf16[32,8,128]{2,1,0:T(8,128)(2,1)S(1)}, u32[]{:S(2)}, u32[]{:S(2)}) async-start(bf16[32,8,128]{2,1,0:T(8,128)(2,1)} %x_solve.1.after_ref), calls=%async_computation.1 | async-start | bytes 131072 | tf_op jit(solution)/shard_map/all_to_all | solution.py:396
  49.8 0.0 copy-done.5
  49.8 0.0 copy-done.6
  49.9 0.0 copy-done.2
  49.9 0.7 %y_solve.1.coef_ref = bf16[8,1536]{1,0:T(8,128)(2,1)S(1)} custom-call(bf16[16,104,128]{2,1,0:T(8,128)(2,1)S(1)} %all_gather.3.r_ref, f32[2,32,32]{2,1,0:T(8,128)S(1)} %copy-done.2), custom_call_target="tpu_custom_call" | custom-call | flops 100000000 | bytes 434176 | tf_op jit(solution)/shard_map/y_solve/pallas_call | solution.py:342
  50.6 0.0 copy-done.3
  50.6 0.0 copy-done.4
  50.6 3.7 %own.1 = (f32[12,264,128]{2,1,0:T(8,128)S(1)}, bf16[16,256]{1,0:T(8,128)(2,1)S(1)}, f32[8,128]{1,0:T(8,128)S(1)}, bf16[4,264,128]{2,1,0:T(8,128)(2,1)S(1)}) custom-call(s32[8,128]{1,0:T(8,128)S(1)} %get-tuple-element.15.count_ref, bf16[12,264,128]{2,1,0:T(8,128)(2,1)} %bitcast.15, bf16[264,128]{1,0:T(8,128)(2,1)S(1)} %get-tuple-element.17.x_ref, ...), custom_call_target="tpu_custom_call" | custom-call | flops 600000000 | bytes 1271488 | tf_op jit(solution)/shard_map/own/pallas_call | solution.py:342
  54.3 4.4 %all-to-all-done.1.c_ref = bf16[32,8,128]{2,1,0:T(8,128)(2,1)S(1)} async-done(((bf16[32,8,128]{2,1,0:T(8,128)(2,1)}), bf16[32,8,128]{2,1,0:T(8,128)(2,1)S(1)}, u32[]{:S(2)}, u32[]{:S(2)}) %all-to-all-start.1) | async-done | bytes 65568 | tf_op jit(solution)/shard_map/all_to_all | solution.py:396
  58.7 0.0 copy-done
  58.7 1.9 %finish.1 = (bf16[12,264,128]{2,1,0:T(8,128)(2,1)}, bf16[12,264,128]{2,1,0:T(8,128)(2,1)}) custom-call(s32[8,128]{1,0:T(8,128)S(1)} %get-tuple-element.15.count_ref, bf16[32,8,128]{2,1,0:T(8,128)(2,1)S(1)} %all-to-all-done.1.c_ref, bf16[4,264,128]{2,1,0:T(8,128)(2,1)S(1)} %get-tuple-element.22.v_ref, bf16[12,264,128]{2,1,0:T(8,128)(2,1)S(1)} %bitcast.11, ...), custom_call_target="tpu_custom_call" | custom-call | flops 100000000 | bytes 2785280 | tf_op jit(solution)/shard_map/finish/pallas_call | solution.py:342
  (3 shorter events, 0.0 us)
Async XLA Ops:
  0.6 38.7 %copy-start.1 = (f32[2,64,64]{2,1,0:T(8,128)S(1)}, f32[2,64,64]{2,1,0:T(8,128)}, u32[]{:S(2)}) copy-start(f32[2,64,64]{2,1,0:T(8,128)} %coupling_ref.2) | copy-start | bytes 98308
  3.0 46.8 %copy-start.5 = (f32[1,2,2,264]{3,2,1,0:T(2,128)S(1)}, f32[1,2,2,264]{3,2,1,0:T(2,128)}, u32[]{:S(2)}) copy-start(f32[1,2,2,264]{3,2,1,0:T(2,128)} %param.25) | copy-start | bytes 12676
  3.0 46.9 %copy-start.6 = (f32[2,2,128]{2,1,0:T(2,128)S(1)}, f32[2,2,128]{2,1,0:T(2,128)}, u32[]{:S(2)}) copy-start(f32[2,2,128]{2,1,0:T(2,128)} %param.22) | copy-start | bytes 6148
  3.0 46.9 %copy-start.2 = (f32[2,32,32]{2,1,0:T(8,128)S(1)}, f32[2,32,32]{2,1,0:T(8,128)}, u32[]{:S(2)}) copy-start(f32[2,32,32]{2,1,0:T(8,128)} %coupling_ref.3) | copy-start | bytes 24580
  3.0 47.6 %copy-start.3 = (f32[264]{0:T(512)S(1)}, f32[264]{0:T(512)}, u32[]{:S(2)}) copy-start(f32[264]{0:T(512)} %yc_ref.1) | copy-start | bytes 3172
  3.0 47.6 %copy-start.4 = (f32[128]{0:T(128)S(1)}, f32[128]{0:T(128)}, u32[]{:S(2)}) copy-start(f32[128]{0:T(128)} %param.17) | copy-start | bytes 1540
  3.0 36.3 %all-to-all-start = ((bf16[32,8,128]{2,1,0:T(8,128)(2,1)}), bf16[32,8,128]{2,1,0:T(8,128)(2,1)S(1)}, u32[]{:S(2)}, u32[]{:S(2)}) async-start(bf16[32,8,128]{2,1,0:T(8,128)(2,1)} %get-tuple-element.16), calls=%async_computation | async-start | bytes 131072 | tf_op jit(solution)/shard_map/all_to_all | solution.py:384
  39.3 19.3 %copy-start = (bf16[3,4,264,128]{3,2,1,0:T(8,128)(2,1)S(1)}, bf16[3,4,264,128]{3,2,1,0:T(8,128)(2,1)}, u32[]{:S(2)}) copy-start(bf16[3,4,264,128]{3,2,1,0:T(8,128)(2,1)} %param.14) | copy-start | bytes 2433028
  40.3 18.4 %all-to-all-start.1 = ((bf16[32,8,128]{2,1,0:T(8,128)(2,1)}), bf16[32,8,128]{2,1,0:T(8,128)(2,1)S(1)}, u32[]{:S(2)}, u32[]{:S(2)}) async-start(bf16[32,8,128]{2,1,0:T(8,128)(2,1)} %x_solve.1.after_ref), calls=%async_computation.1 | async-start | bytes 131072 | tf_op jit(solution)/shard_map/all_to_all | solution.py:396
